TPU v7x, 128 devices: a whole 4x4x4 slice. The times are simulated.
128 devices in a mesh: lat: 4 (over x_hi, core), lon: 32 (over y, z, x_lo).
Axes of the slice: x: 4 (x_hi: 2, x_lo: 2; x = x_hi * 2 + x_lo), y: 4, z: 4, core: 2. Of those that a mesh axis runs over, the one named last changes fastest.
Arguments:
- starting_vector: bfloat16 [256, 3584, 128], P('lat', 'lon'), may hold values from -6 to 6
- conv_first: bfloat16 [3, 3, 128, 128], replicated, may hold values from -0.1875 to 0.1875
- later_stencil_matrix: bfloat16 [3, 3, 128, 128], replicated, may hold values from -0.1875 to 0.1875
- obs_in: bfloat16 [128, 512], replicated, may hold values from -0.5 to 0.5
- obs_bias: float32 [512], replicated, may hold values from -3 to 3
- obs_out: bfloat16 [512, 256], replicated, may hold values from -0.25 to 0.25
- innovations: bfloat16 [128, 32, 128, 256], P(('lat', 'lon')), may hold values from -6 to 6
- counts: int32 [128, 32], P(('lat', 'lon')), may hold values from 1 to 128, as said below
- columns: int32 [128, 32, 128], P(('lat', 'lon')), may hold values from 0 to 7167
Outputs:
- gradient: float32 [256, 3584, 128], P('lat', 'lon')
Inputs may be any that keep to these rules, and one draw needn't show every extreme that they name: `counts`: in every latitude row of devices one longitude tile, drawn, receives 128 live slots from every source of that row.
All inputs are finite; a program needn't handle non-finite values.
Results may differ from a plain program's by a relative error of at most 0.0049.
Values may be sent and summed in bfloat16 or wider, within the bound.
No kernel may reach another device: no remote copies, remote signals or barrier semaphores. Data moves between devices by JAX's collectives and lax.ppermute only.
A program may use at most 128 MiB of HBM per device.

v0:
```python
import jax
import jax.numpy as jnp
from jax import lax
from jax.experimental import pallas as pl
from jax.experimental.pallas import tpu as pltpu
from jax.sharding import PartitionSpec as P

BF = jnp.bfloat16
F32 = jnp.float32
WIDE = 128
PAD = 136
BLOCK = 512
TOTALS = 4


def sigmoid(value):
    return 0.5 * jnp.tanh(0.5 * value) + 0.5


def pair_weights(kernel_ref, out_ref):
    depth = kernel_ref.shape[-1]
    zero = jnp.zeros((depth, depth), BF)
    for row in range(4):
        for col in range(3):
            at = (row * 3 + col) * depth
            out_ref[at : at + depth, :depth] = kernel_ref[row, col] if row < 3 else zero
            out_ref[at : at + depth, depth:] = kernel_ref[row - 1, col] if row > 0 else zero


def taps_across(source_ref, taps_ref, start, width):
    depth = source_ref.shape[-1]
    for col in range(3):
        taps_ref[:, :, :, col * depth : (col + 1) * depth] = source_ref[
            :, :, start + col : start + col + width, :
        ].astype(BF)


def row_pairs(taps_ref, weights_ref, first, last):
    count, width, wide = last - first, taps_ref.shape[2], taps_ref.shape[3]
    rows = [
        taps_ref[first + a // 2 : last + a // 2, a % 2].reshape(count * width, wide)
        for a in range(4)
    ]
    total = jnp.dot(
        jnp.concatenate(rows, axis=1), weights_ref[...], preferred_element_type=F32
    )
    depth = wide // 3
    return (
        total[:, :depth].reshape(count, width, depth),
        total[:, depth:].reshape(count, width, depth),
    )


def spans(total, pieces):
    cuts = [total * i // pieces for i in range(pieces + 1)]
    return list(zip(cuts[:-1], cuts[1:]))


def pad_field(padded_ref, inner, top_ref, bottom_ref, left_ref, right_ref):
    pairs = padded_ref.shape[0]
    width = top_ref.shape[1]
    padded_ref[1 : pairs - 1, :, 8 : 8 + width, :] = inner
    padded_ref[0, :, 8 : 8 + width, :] = top_ref[...].astype(F32)
    padded_ref[pairs - 1, :, 8 : 8 + width, :] = bottom_ref[...].astype(F32)
    padded_ref[:, :, 6:8, :] = left_ref[...].astype(F32).reshape(pairs, 2, 2, -1)
    padded_ref[:, :, 8 + width : 10 + width, :] = right_ref[...].astype(F32).reshape(
        pairs, 2, 2, -1
    )


def forward_kernel(
    edge_ref, x_ref, top_ref, bottom_ref, left_ref, right_ref, first_ref, second_ref,
    forecast_ref, slope_ref,
    padded, taps_one, hidden, taps_two, weights_one, weights_two,
):
    rows, width, depth = x_ref.shape
    pair_weights(first_ref, weights_one)
    pair_weights(second_ref, weights_two)
    pad_field(
        padded, x_ref[...].astype(F32).reshape(rows // 2, 2, width, depth),
        top_ref, bottom_ref, left_ref, right_ref,
    )
    taps_across(padded, taps_one, 6, WIDE)
    pairs = rows // 2 + 1
    for first, last in spans(pairs, 3):
        for odd, pre in enumerate(row_pairs(taps_one, weights_one, first, last)):
            sig = sigmoid(pre)
            hidden[first:last, odd] = pre * sig
            slope_ref[first:last, odd] = sig * (1.0 + pre * (1.0 - sig))
    hidden[0, 0] = hidden[0, 0] * edge_ref[0]
    hidden[pairs - 1, 1] = hidden[pairs - 1, 1] * edge_ref[1]
    taps_across(hidden, taps_two, 0, width)
    for first, last in spans(rows // 2, 4):
        for odd, change in enumerate(row_pairs(taps_two, weights_two, first, last)):
            for pair in range(first, last):
                row = 2 * pair + odd
                forecast_ref[row] = (
                    (x_ref[row].astype(F32) + change[pair - first]).astype(BF).astype(F32)
                )
    forecast_ref[rows] = jnp.zeros((width, depth), F32)


def observe_kernel(
    cells_ref, forecast_ref, into_ref, bias_ref, out_ref, predicted_ref, slope_ref, state
):
    step = pl.program_id(0)

    def take(slot, carry):
        state[pl.ds(slot, 1), :] = forecast_ref[pl.ds(cells_ref[step * BLOCK + slot], 1), :]
        return carry

    lax.fori_loop(0, BLOCK, take, 0, unroll=16)
    z = jnp.dot(state[...].astype(BF), into_ref[...], preferred_element_type=F32) + bias_ref[...]
    sig = sigmoid(z)
    slope_ref[...] = sig * (1.0 + z * (1.0 - sig))
    predicted_ref[...] = jnp.dot(
        (z * sig).astype(BF), out_ref[...], preferred_element_type=F32
    )


def scatter_kernel(
    cells_ref, radiance_ref, predicted_ref, slope_ref, out_t_ref, into_t_ref,
    total_ref, rim_ref, side_ref, grads, *parts,
):
    step = pl.program_id(0)

    @pl.when(step == 0)
    def _():
        for part in parts:
            part[...] = jnp.zeros(part.shape, F32)

    misfit = (predicted_ref[...] - radiance_ref[...].astype(F32)).astype(BF)
    back = jnp.dot(misfit, out_t_ref[...], preferred_element_type=F32)
    grads[...] = jnp.dot(
        (back * slope_ref[...]).astype(BF), into_t_ref[...], preferred_element_type=F32
    )

    def add(group, carry):
        for k, part in enumerate(parts):
            slot = group * len(parts) + k
            at = pl.ds(cells_ref[step * BLOCK + slot], 1)
            part[at, :] = part[at, :] + grads[pl.ds(slot, 1), :]
        return carry

    lax.fori_loop(0, BLOCK // len(parts), add, 0, unroll=4)

    @pl.when(step == pl.num_programs(0) - 1)
    def _():
        rows, width, depth = total_ref.shape
        total = parts[0][: rows * width]
        for part in parts[1:]:
            total = total + part[: rows * width]
        total = total.reshape(rows, width, depth)
        total_ref[...] = total
        rim_ref[0] = total[:2].astype(BF)
        rim_ref[1] = total[rows - 2 :].astype(BF)
        side_ref[0] = total_ref[:, 0:2, :].astype(BF)
        side_ref[1] = total_ref[:, width - 2 : width, :].astype(BF)


def backward_kernel(
    edge_ref, d_ref, top_ref, bottom_ref, left_ref, right_ref, second_ref, first_ref, slope_ref,
    out_ref,
    padded, taps_one, change, taps_two, weights_one, weights_two,
):
    rows, width, depth = d_ref.shape
    pair_weights(second_ref, weights_one)
    pair_weights(first_ref, weights_two)
    pad_field(
        padded, d_ref[...].reshape(rows // 2, 2, width, depth),
        top_ref, bottom_ref, left_ref, right_ref,
    )
    taps_across(padded, taps_one, 6, WIDE)
    pairs = rows // 2 + 1
    for first, last in spans(pairs, 3):
        for odd, dhidden in enumerate(row_pairs(taps_one, weights_one, first, last)):
            change[first:last, odd] = dhidden * slope_ref[first:last, odd]
    change[0, 0] = change[0, 0] * edge_ref[0]
    change[pairs - 1, 1] = change[pairs - 1, 1] * edge_ref[1]
    taps_across(change, taps_two, 0, width)
    for first, last in spans(rows // 2, 4):
        for odd, back in enumerate(row_pairs(taps_two, weights_two, first, last)):
            for pair in range(first, last):
                row = 2 * pair + odd
                out_ref[row] = d_ref[row] + back[pair - first]


VMEM = pl.BlockSpec(memory_space=pltpu.VMEM)
SMEM = pl.BlockSpec(memory_space=pltpu.SMEM)


def params(**more):
    return pltpu.CompilerParams(vmem_limit_bytes=60 * 1024 * 1024, **more)


def conv_scratch(rows, width, depth):
    return [
        pltpu.VMEM((rows // 2 + 2, 2, PAD, depth), F32),
        pltpu.VMEM((rows // 2 + 2, 2, WIDE, 3 * depth), BF),
        pltpu.VMEM((rows // 2 + 1, 2, WIDE, depth), F32),
        pltpu.VMEM((rows // 2 + 1, 2, width, 3 * depth), BF),
        pltpu.VMEM((12 * depth, 2 * depth), BF),
        pltpu.VMEM((12 * depth, 2 * depth), BF),
    ]


def flipped(kernel):
    return jnp.transpose(kernel[::-1, ::-1], (0, 1, 3, 2))


def shifted(array, axis, step, wrap):
    count = lax.axis_size(axis)
    return lax.ppermute(
        array, axis, [(i, (i + step) % count) for i in range(count) if wrap or 0 <= i + step < count]
    )


def border(head, tail, left, right):
    top = shifted(tail, "lat", 1, False)
    bottom = shifted(head, "lat", -1, False)
    left = jnp.concatenate([top[:, :2], left, bottom[:, :2]], axis=0)
    right = jnp.concatenate([top[:, -2:], right, bottom[:, -2:]], axis=0)
    return top, bottom, shifted(right, "lon", 1, True), shifted(left, "lon", -1, True)


def per_device(
    starting_vector, conv_first, later_stencil_matrix, obs_in, obs_bias, obs_out,
    innovations, counts, columns,
):
    rows, width, depth = starting_vector.shape
    lon_count, slots, channels = innovations.shape[1:]
    hidden_units = obs_in.shape[1]
    taken = lon_count * slots
    lat = lax.axis_index("lat")
    edge = jnp.stack([lat > 0, lat < lax.axis_size("lat") - 1]).astype(F32)

    live = lax.iota(jnp.int32, slots)[None, :] < counts[0][:, None]
    cells = jnp.where(live, columns[0], rows * width)
    cells = lax.all_to_all(cells, "lon", 0, 0, tiled=True).reshape(-1)
    radiance = lax.all_to_all(innovations[0], "lon", 0, 0, tiled=True).reshape(taken, channels)

    x = starting_vector
    ring = border(x[:2], x[-2:], x[:, :2], x[:, -2:])
    pairs = rows // 2 + 1
    forecast, slope = pl.pallas_call(
        forward_kernel,
        out_shape=(
            jax.ShapeDtypeStruct((rows + 1, width, depth), F32),
            jax.ShapeDtypeStruct((pairs, 2, WIDE, depth), F32),
        ),
        in_specs=[SMEM] + [VMEM] * 7,
        out_specs=(VMEM, VMEM),
        scratch_shapes=conv_scratch(rows, width, depth),
        compiler_params=params(),
        name="forward",
    )(edge, x, *ring, conv_first, later_stencil_matrix)

    predicted, z_slope = pl.pallas_call(
        observe_kernel,
        grid=(taken // BLOCK,),
        out_shape=(
            jax.ShapeDtypeStruct((taken, channels), F32),
            jax.ShapeDtypeStruct((taken, hidden_units), F32),
        ),
        in_specs=[SMEM] + [VMEM] * 4,
        out_specs=(
            pl.BlockSpec((BLOCK, channels), lambda i: (i, 0)),
            pl.BlockSpec((BLOCK, hidden_units), lambda i: (i, 0)),
        ),
        scratch_shapes=[pltpu.VMEM((BLOCK, depth), F32)],
        compiler_params=params(),
        name="observe",
    )(cells, forecast.reshape((rows + 1) * width, depth), obs_in, obs_bias[None], obs_out)

    dforecast, rim, side = pl.pallas_call(
        scatter_kernel,
        grid=(taken // BLOCK,),
        out_shape=(
            jax.ShapeDtypeStruct((rows, width, depth), F32),
            jax.ShapeDtypeStruct((2, 2, width, depth), BF),
            jax.ShapeDtypeStruct((2, rows, 2, depth), BF),
        ),
        in_specs=[
            SMEM,
            pl.BlockSpec((BLOCK, channels), lambda i: (i, 0)),
            pl.BlockSpec((BLOCK, channels), lambda i: (i, 0)),
            pl.BlockSpec((BLOCK, hidden_units), lambda i: (i, 0)),
            VMEM,
            VMEM,
        ],
        out_specs=(VMEM, VMEM, VMEM),
        scratch_shapes=[pltpu.VMEM((BLOCK, depth), F32)]
        + [pltpu.VMEM((rows * width + 8, depth), F32)] * TOTALS,
        compiler_params=params(),
        name="scatter",
    )(cells, radiance, predicted, z_slope, obs_out.T, obs_in.T)

    ring = border(rim[0], rim[1], side[0], side[1])
    return pl.pallas_call(
        backward_kernel,
        out_shape=jax.ShapeDtypeStruct((rows, width, depth), F32),
        in_specs=[SMEM] + [VMEM] * 8,
        out_specs=VMEM,
        scratch_shapes=conv_scratch(rows, width, depth),
        compiler_params=params(),
        name="backward",
    )(edge, dforecast, *ring, flipped(later_stencil_matrix), flipped(conv_first), slope)


def solution(mesh):
    placed = (
        P("lat", "lon", None),
        P(),
        P(),
        P(),
        P(),
        P(),
        P(("lat", "lon"), None, None, None),
        P(("lat", "lon"), None),
        P(("lat", "lon"), None, None),
    )
    return jax.shard_map(
        per_device, mesh=mesh, in_specs=placed, out_specs=P("lat", "lon", None), check_vma=False
    )
```

profile of v0, /device:TPU:1, one launch (start us, length us, event | category | flops | bytes accessed | tf_op | source)
XLA Modules:
  0.0 142.9 jit_solution(17443743451076605657)
XLA Ops:
  0.0 0.0 copy-start.1
  0.0 0.9 compare_select_fusion
  0.9 16.7 %all_to_all.11 = s32[32,1,128]{2,1,0:T(1,128)} all-to-all(s32[32,1,128]{2,1,0:T(1,128)S(1)} %compare_select_fusion), channel_id=1, replica_groups=mesh['lat'=4,'lon'=32] {'lon'}, dimensions={0} | all-to-all | bytes 32768 | tf_op jit(solution)/shard_map/all_to_all | solution.py:239
  17.6 4.0 %all-to-all-start.1 = ((bf16[32,128,256]{2,1,0:T(8,128)(2,1)}), bf16[32,128,256]{2,1,0:T(8,128)(2,1)S(1)}, u32[]{:S(2)}, u32[]{:S(2)}) async-start(bf16[32,128,256]{2,1,0:T(8,128)(2,1)} %bitcast.25), calls=%async_computation.1 | async-start | bytes 4194304 | tf_op jit(solution)/shard_map/all_to_all | solution.py:240
  21.7 0.9 fusion.1
  22.5 6.4 %collective-permute-start = (bf16[2,112,128]{2,1,0:T(8,128)(2,1)S(1)}, bf16[2,112,128]{2,1,0:T(8,128)(2,1)S(1)}, u32[]{:S(2)}, u32[]{:S(2)}) collective-permute-start(bf16[2,112,128]{2,1,0:T(8,128)(2,1)S(1)} %get-tuple-element.22), channel_id=1, source_target_pairs={{0,32},{32,64},{64,96},{1,33},{33,65},{65,97},{2,34},{34,66},{66,9... | collective-permute-start | bytes 172040 | tf_op jit(solution)/shard_map/ppermute | solution.py:213
  29.0 1.9 %collective-permute-start.1 = (bf16[2,112,128]{2,1,0:T(8,128)(2,1)S(1)}, bf16[2,112,128]{2,1,0:T(8,128)(2,1)S(1)}, u32[]{:S(2)}, u32[]{:S(2)}) collective-permute-start(bf16[2,112,128]{2,1,0:T(8,128)(2,1)S(1)} %get-tuple-element.21), channel_id=1, source_target_pairs={{32,0},{64,32},{96,64},{33,1},{65,33},{97,65},{34,2},{66,34},{98,6... | collective-permute-start | bytes 172040 | tf_op jit(solution)/shard_map/ppermute | solution.py:213
  30.9 1.0 fusion
  31.9 12.2 %collective-permute-done.top_ref = bf16[2,112,128]{2,1,0:T(8,128)(2,1)S(1)} collective-permute-done((bf16[2,112,128]{2,1,0:T(8,128)(2,1)S(1)}, bf16[2,112,128]{2,1,0:T(8,128)(2,1)S(1)}, u32[]{:S(2)}, u32[]{:S(2)}) %collective-permute-start) | collective-permute-done | bytes 57376 | tf_op jit(solution)/shard_map/ppermute | solution.py:213
  44.1 5.4 %collective-permute-done.1.bottom_ref = bf16[2,112,128]{2,1,0:T(8,128)(2,1)S(1)} collective-permute-done((bf16[2,112,128]{2,1,0:T(8,128)(2,1)S(1)}, bf16[2,112,128]{2,1,0:T(8,128)(2,1)S(1)}, u32[]{:S(2)}, u32[]{:S(2)}) %collective-permute-start.1) | collective-permute-done | bytes 57376 | tf_op jit(solution)/shard_map/ppermute | solution.py:213
  49.6 0.1 pad_maximum_fusion.1
  49.6 7.5 %collective-permute-start.3 = (bf16[68,2,128]{2,1,0:T(2,128)(2,1)S(1)}, bf16[68,2,128]{2,1,0:T(2,128)(2,1)}, u32[]{:S(2)}, u32[]{:S(2)}) collective-permute-start(bf16[68,2,128]{2,1,0:T(2,128)(2,1)S(1)} %pad_maximum_fusion.1), channel_id=1, source_target_pairs={{0,31},{1,0},{2,1},{3,2},{4,3},{5,4},{6,5},{7,6},{8,7},{9,8},{10,9... | collective-permute-start | bytes 104456 | tf_op jit(solution)/shard_map/ppermute | solution.py:213
  57.1 0.7 pad_maximum_fusion
  57.8 0.0 collective-permute-start.2
  57.8 0.6 add_convert_fusion.edge_ref
  58.4 0.0 copy-done.3
  58.4 0.8 copy.14
  59.2 0.0 copy-done.4
  59.2 0.8 copy.15
  60.0 0.0 copy-done.2
  60.0 0.2 copy.16
  60.2 0.0 copy-done.1
  60.2 0.2 copy.17
  60.4 0.0 collective-permute-done.3.right_ref
  60.4 4.7 %collective-permute-done.2.left_ref = bf16[68,2,128]{2,1,0:T(2,128)(2,1)} collective-permute-done((bf16[68,2,128]{2,1,0:T(2,128)(2,1)}, bf16[68,2,128]{2,1,0:T(2,128)(2,1)}, u32[]{:S(2)}, u32[]{:S(2)}) %collective-permute-start.2) | collective-permute-done | bytes 34848 | tf_op jit(solution)/shard_map/ppermute | solution.py:213
  65.1 0.0 copy-done.6
  65.1 12.1 %forward.1 = (f32[65,112,128]{2,1,0:T(8,128)}, f32[33,2,128,128]{3,2,1,0:T(8,128)}) custom-call(f32[2]{0:T(128)} %add_convert_fusion.edge_ref, bf16[64,112,128]{2,1,0:T(8,128)(2,1)} %x_ref.1, bf16[2,112,128]{2,1,0:T(8,128)(2,1)} %copy-done.5, bf16[2,112,128]{2,1,0:T(8,128)(2,1)} %copy-done.6, bf16[68,2,128]{2,1,0:T(2,128)(2,1)} %collective-permute-done.2.left_ref, ...), custom_call_target="tpu_custom_call" | custom-call | tf_op jit(solution)/shard_map/forward/pallas_call | solution.py:245
  77.2 14.5 %observe.1 = (f32[4096,256]{1,0:T(8,128)}, f32[4096,512]{1,0:T(8,128)}) custom-call(s32[4096]{0:T(1024)} %bitcast.28, f32[7280,128]{1,0:T(8,128)} %bitcast.24, bf16[128,512]{1,0:T(8,128)(2,1)} %into_ref.1, f32[1,512]{1,0:T(1,128)} %bitcast.31, bf16[512,256]{1,0:T(8,128)(2,1)} %out_ref.1), custom_call_target="tpu_custom_call" | custom-call | tf_op jit(solution)/shard_map/observe/pallas_call | solution.py:258
  91.7 0.0 all-to-all-done.1
  91.7 1.3 copy-done
  93.0 17.0 %scatter.1 = (f32[64,112,128]{2,1,0:T(8,128)}, bf16[2,2,112,128]{3,2,1,0:T(8,128)(2,1)}, bf16[2,64,2,128]{3,2,1,0:T(2,128)(2,1)}) custom-call(s32[4096]{0:T(1024)} %bitcast.29, bf16[4096,256]{1,0:T(8,128)(2,1)} %bitcast.23, f32[4096,256]{1,0:T(8,128)} %get-tuple-element.13.predicted_ref, f32[4096,512]{1,0:T(8,128)} %get-tuple-element.14.slope_ref, ...), custom_call_target="tpu_custom_call" | custom-call | tf_op jit(solution)/shard_map/scatter/pallas_call | solution.py:275
  110.0 0.9 slice_bitcast_fusion
  110.9 3.8 %collective-permute-start.4 = (bf16[2,112,128]{2,1,0:T(8,128)(2,1)S(1)}, bf16[2,112,128]{2,1,0:T(8,128)(2,1)S(1)}, u32[]{:S(2)}, u32[]{:S(2)}) collective-permute-start(bf16[2,112,128]{2,1,0:T(8,128)(2,1)S(1)} %get-tuple-element.24), channel_id=1, source_target_pairs={{0,32},{32,64},{64,96},{1,33},{33,65},{65,97},{2,34},{34,66},{66,9... | collective-permute-start | bytes 172040 | tf_op jit(solution)/shard_map/ppermute | solution.py:213
  114.6 1.9 %collective-permute-start.5 = (bf16[2,112,128]{2,1,0:T(8,128)(2,1)S(1)}, bf16[2,112,128]{2,1,0:T(8,128)(2,1)S(1)}, u32[]{:S(2)}, u32[]{:S(2)}) collective-permute-start(bf16[2,112,128]{2,1,0:T(8,128)(2,1)S(1)} %get-tuple-element.23), channel_id=1, source_target_pairs={{32,0},{64,32},{96,64},{33,1},{65,33},{97,65},{34,2},{66,34},{98,6... | collective-permute-start | bytes 172040 | tf_op jit(solution)/shard_map/ppermute | solution.py:213
  116.6 0.8 slice_bitcast_fusion.2
  117.4 0.0 collective-permute-done.4.top_ref
  117.4 0.0 copy-start.7
  117.4 4.2 %collective-permute-done.5.bottom_ref = bf16[2,112,128]{2,1,0:T(8,128)(2,1)S(1)} collective-permute-done((bf16[2,112,128]{2,1,0:T(8,128)(2,1)S(1)}, bf16[2,112,128]{2,1,0:T(8,128)(2,1)S(1)}, u32[]{:S(2)}, u32[]{:S(2)}) %collective-permute-start.5) | collective-permute-done | bytes 57376 | tf_op jit(solution)/shard_map/ppermute | solution.py:213
  121.6 0.1 pad_maximum_fusion.3
  121.7 0.1 collective-permute-start.7
  121.8 0.1 pad_maximum_fusion.2
  121.8 1.7 %collective-permute-start.6 = (bf16[68,2,128]{2,1,0:T(2,128)(2,1)S(1)}, bf16[68,2,128]{2,1,0:T(2,128)(2,1)S(1)}, u32[]{:S(2)}, u32[]{:S(2)}) collective-permute-start(bf16[68,2,128]{2,1,0:T(2,128)(2,1)S(1)} %pad_maximum_fusion.2), channel_id=1, source_target_pairs={{0,1},{1,2},{2,3},{3,4},{4,5},{5,6},{6,7},{7,8},{8,9},{9,10},{10,1... | collective-permute-start | bytes 104456 | tf_op jit(solution)/shard_map/ppermute | solution.py:213
  123.5 0.9 reverse_bitcast_fusion
  124.4 0.4 collective-permute-done.7.right_ref
  124.9 4.2 %collective-permute-done.6.left_ref = bf16[68,2,128]{2,1,0:T(2,128)(2,1)S(1)} collective-permute-done((bf16[68,2,128]{2,1,0:T(2,128)(2,1)S(1)}, bf16[68,2,128]{2,1,0:T(2,128)(2,1)S(1)}, u32[]{:S(2)}, u32[]{:S(2)}) %collective-permute-start.6) | collective-permute-done | bytes 34848 | tf_op jit(solution)/shard_map/ppermute | solution.py:213
  129.1 0.0 copy-done.8
  129.1 0.6 copy-done.10
  129.7 13.2 %backward.1 = f32[64,112,128]{2,1,0:T(8,128)} custom-call(f32[2]{0:T(128)} %add_convert_fusion.edge_ref, f32[64,112,128]{2,1,0:T(8,128)} %get-tuple-element.15.d_ref, bf16[2,112,128]{2,1,0:T(8,128)(2,1)} %copy-done.7, bf16[2,112,128]{2,1,0:T(8,128)(2,1)} %copy-done.8, bf16[68,2,128]{2,1,0:T(2,128)(2,1)} %copy-done.10, bf16[68,2,128]{2,1,0:T(2,128)(2,1)} %copy-done.9, ...), custom_call_target="tpu_custom_call" | custom-call | tf_op jit(solution)/shard_map/backward/pallas_call | solution.py:299
  (16 shorter events, 0.0 us)
Async XLA Ops:
  0.0 58.4 %copy-start.3 = (bf16[512,256]{1,0:T(8,128)(2,1)S(1)}, bf16[512,256]{1,0:T(8,128)(2,1)}, u32[]{:S(2)}) copy-start(bf16[512,256]{1,0:T(8,128)(2,1)} %out_ref.1) | copy-start | bytes 786436
  0.0 59.2 %copy-start.4 = (bf16[128,512]{1,0:T(8,128)(2,1)S(1)}, bf16[128,512]{1,0:T(8,128)(2,1)}, u32[]{:S(2)}) copy-start(bf16[128,512]{1,0:T(8,128)(2,1)} %into_ref.1) | copy-start | bytes 393220
  0.0 60.0 %copy-start.2 = (bf16[3,3,128,128]{3,2,1,0:T(8,128)(2,1)S(1)}, bf16[3,3,128,128]{3,2,1,0:T(8,128)(2,1)}, u32[]{:S(2)}) copy-start(bf16[3,3,128,128]{3,2,1,0:T(8,128)(2,1)} %second_ref.1) | copy-start | bytes 884740
  0.0 60.2 %copy-start.1 = (bf16[3,3,128,128]{3,2,1,0:T(8,128)(2,1)S(1)}, bf16[3,3,128,128]{3,2,1,0:T(8,128)(2,1)}, u32[]{:S(2)}) copy-start(bf16[3,3,128,128]{3,2,1,0:T(8,128)(2,1)} %first_ref.1) | copy-start | bytes 884740
  17.6 74.1 %all-to-all-start.1 = ((bf16[32,128,256]{2,1,0:T(8,128)(2,1)}), bf16[32,128,256]{2,1,0:T(8,128)(2,1)S(1)}, u32[]{:S(2)}, u32[]{:S(2)}) async-start(bf16[32,128,256]{2,1,0:T(8,128)(2,1)} %bitcast.25), calls=%async_computation.1 | async-start | bytes 4194304 | tf_op jit(solution)/shard_map/all_to_all | solution.py:240
  22.5 21.6 %collective-permute-start = (bf16[2,112,128]{2,1,0:T(8,128)(2,1)S(1)}, bf16[2,112,128]{2,1,0:T(8,128)(2,1)S(1)}, u32[]{:S(2)}, u32[]{:S(2)}) collective-permute-start(bf16[2,112,128]{2,1,0:T(8,128)(2,1)S(1)} %get-tuple-element.22), channel_id=1, source_target_pairs={{0,32},{32,64},{64,96},{1,33},{33,65},{65,97},{2,34},{34,66},{66,9... | collective-permute-start | bytes 172040 | tf_op jit(solution)/shard_map/ppermute | solution.py:213
  29.0 20.6 %collective-permute-start.1 = (bf16[2,112,128]{2,1,0:T(8,128)(2,1)S(1)}, bf16[2,112,128]{2,1,0:T(8,128)(2,1)S(1)}, u32[]{:S(2)}, u32[]{:S(2)}) collective-permute-start(bf16[2,112,128]{2,1,0:T(8,128)(2,1)S(1)} %get-tuple-element.21), channel_id=1, source_target_pairs={{32,0},{64,32},{96,64},{33,1},{65,33},{97,65},{34,2},{66,34},{98,6... | collective-permute-start | bytes 172040 | tf_op jit(solution)/shard_map/ppermute | solution.py:213
  44.1 21.0 %copy-start.5 = (bf16[2,112,128]{2,1,0:T(8,128)(2,1)}, bf16[2,112,128]{2,1,0:T(8,128)(2,1)S(1)}, u32[]{:S(2)}) copy-start(bf16[2,112,128]{2,1,0:T(8,128)(2,1)S(1)} %collective-permute-done.top_ref) | copy-start | bytes 172036
  49.6 15.5 %copy-start.6 = (bf16[2,112,128]{2,1,0:T(8,128)(2,1)}, bf16[2,112,128]{2,1,0:T(8,128)(2,1)S(1)}, u32[]{:S(2)}) copy-start(bf16[2,112,128]{2,1,0:T(8,128)(2,1)S(1)} %collective-permute-done.1.bottom_ref) | copy-start | bytes 172036
  49.6 10.8 %collective-permute-start.3 = (bf16[68,2,128]{2,1,0:T(2,128)(2,1)S(1)}, bf16[68,2,128]{2,1,0:T(2,128)(2,1)}, u32[]{:S(2)}, u32[]{:S(2)}) collective-permute-start(bf16[68,2,128]{2,1,0:T(2,128)(2,1)S(1)} %pad_maximum_fusion.1), channel_id=1, source_target_pairs={{0,31},{1,0},{2,1},{3,2},{4,3},{5,4},{6,5},{7,6},{8,7},{9,8},{10,9... | collective-permute-start | bytes 104456 | tf_op jit(solution)/shard_map/ppermute | solution.py:213
  57.8 7.3 %collective-permute-start.2 = (bf16[68,2,128]{2,1,0:T(2,128)(2,1)}, bf16[68,2,128]{2,1,0:T(2,128)(2,1)}, u32[]{:S(2)}, u32[]{:S(2)}) collective-permute-start(bf16[68,2,128]{2,1,0:T(2,128)(2,1)} %pad_maximum_fusion), channel_id=1, source_target_pairs={{0,1},{1,2},{2,3},{3,4},{4,5},{5,6},{6,7},{7,8},{8,9},{9,10},{10,1... | collective-permute-start | bytes 104456 | tf_op jit(solution)/shard_map/ppermute | solution.py:213
  91.7 1.3 copy-start
  110.9 6.5 %collective-permute-start.4 = (bf16[2,112,128]{2,1,0:T(8,128)(2,1)S(1)}, bf16[2,112,128]{2,1,0:T(8,128)(2,1)S(1)}, u32[]{:S(2)}, u32[]{:S(2)}) collective-permute-start(bf16[2,112,128]{2,1,0:T(8,128)(2,1)S(1)} %get-tuple-element.24), channel_id=1, source_target_pairs={{0,32},{32,64},{64,96},{1,33},{33,65},{65,97},{2,34},{34,66},{66,9... | collective-permute-start | bytes 172040 | tf_op jit(solution)/shard_map/ppermute | solution.py:213
  114.6 7.0 %collective-permute-start.5 = (bf16[2,112,128]{2,1,0:T(8,128)(2,1)S(1)}, bf16[2,112,128]{2,1,0:T(8,128)(2,1)S(1)}, u32[]{:S(2)}, u32[]{:S(2)}) collective-permute-start(bf16[2,112,128]{2,1,0:T(8,128)(2,1)S(1)} %get-tuple-element.23), channel_id=1, source_target_pairs={{32,0},{64,32},{96,64},{33,1},{65,33},{97,65},{34,2},{66,34},{98,6... | collective-permute-start | bytes 172040 | tf_op jit(solution)/shard_map/ppermute | solution.py:213
  117.4 11.7 %copy-start.7 = (bf16[2,112,128]{2,1,0:T(8,128)(2,1)}, bf16[2,112,128]{2,1,0:T(8,128)(2,1)S(1)}, u32[]{:S(2)}) copy-start(bf16[2,112,128]{2,1,0:T(8,128)(2,1)S(1)} %collective-permute-done.4.top_ref) | copy-start | bytes 172036
  121.6 7.5 %copy-start.8 = (bf16[2,112,128]{2,1,0:T(8,128)(2,1)}, bf16[2,112,128]{2,1,0:T(8,128)(2,1)S(1)}, u32[]{:S(2)}) copy-start(bf16[2,112,128]{2,1,0:T(8,128)(2,1)S(1)} %collective-permute-done.5.bottom_ref) | copy-start | bytes 172036
  121.7 3.2 %collective-permute-start.7 = (bf16[68,2,128]{2,1,0:T(2,128)(2,1)S(1)}, bf16[68,2,128]{2,1,0:T(2,128)(2,1)S(1)}, u32[]{:S(2)}, u32[]{:S(2)}) collective-permute-start(bf16[68,2,128]{2,1,0:T(2,128)(2,1)S(1)} %pad_maximum_fusion.3), channel_id=1, source_target_pairs={{0,31},{1,0},{2,1},{3,2},{4,3},{5,4},{6,5},{7,6},{8,7},{9,8},{10,9... | collective-permute-start | bytes 104456 | tf_op jit(solution)/shard_map/ppermute | solution.py:213
  121.8 7.3 %collective-permute-start.6 = (bf16[68,2,128]{2,1,0:T(2,128)(2,1)S(1)}, bf16[68,2,128]{2,1,0:T(2,128)(2,1)S(1)}, u32[]{:S(2)}, u32[]{:S(2)}) collective-permute-start(bf16[68,2,128]{2,1,0:T(2,128)(2,1)S(1)} %pad_maximum_fusion.2), channel_id=1, source_target_pairs={{0,1},{1,2},{2,3},{3,4},{4,5},{5,6},{6,7},{7,8},{8,9},{9,10},{10,1... | collective-permute-start | bytes 104456 | tf_op jit(solution)/shard_map/ppermute | solution.py:213
  124.9 4.3 %copy-start.9 = (bf16[68,2,128]{2,1,0:T(2,128)(2,1)}, bf16[68,2,128]{2,1,0:T(2,128)(2,1)S(1)}, u32[]{:S(2)}) copy-start(bf16[68,2,128]{2,1,0:T(2,128)(2,1)S(1)} %collective-permute-done.7.right_ref) | copy-start | bytes 104452
  129.1 0.6 copy-start.10
where the time goes:
time: 144 us; the launch traced here: 143 us
  Pallas kernels  56.7 us (39%)
  waiting for transfers between devices  31.2 us (22%)
  starting transfers between devices  27.3 us (19%)
  blocking collectives  16.7 us (12%)
  local copies, waits for them, and re-layouts  8.46 us (6%)
  other arithmetic  2.32 us (2%)
    ppermute x8, waiting for transfers between devices, shifted(): lax.ppermute(array, axis, [(i, (i + step) % count) for i in range(count)...  31.2 us
    ppermute x8, starting transfers between devices, shifted(): lax.ppermute(array, axis, [(i, (i + step) % count) for i in range(count)...  23.3 us
    pallas_call x1, Pallas kernels, per_device(): pl.pallas_call(scatter_kernel, grid=(taken // BLOCK,), out_shape=(jax.Sha...  17 us
    all_to_all x1, blocking collectives, per_device(): cells = lax.all_to_all(cells, 'lon', 0, 0, tiled=True).reshape(-1)  16.7 us
    pallas_call x1, Pallas kernels, per_device(): pl.pallas_call(observe_kernel, grid=(taken // BLOCK,), out_shape=(jax.Sha...  14.5 us
    pallas_call x1, Pallas kernels, per_device(): pl.pallas_call(backward_kernel, out_shape=jax.ShapeDtypeStruct((rows, wid...  13.2 us
    pallas_call x1, Pallas kernels, per_device(): pl.pallas_call(forward_kernel, out_shape=(jax.ShapeDtypeStruct((rows + 1,...  12.1 us
    all_to_all x1, starting transfers between devices, per_device(): lax.all_to_all(innovations[0], 'lon', 0, 0, tiled=True)  4.01 us
  transfers between devices with their start and end apart: 9, of which 6 were waited for; matrix products, arithmetic and copies ran while one was open for 5% of the time, Pallas kernels for 19%

commit v1 on v0

v1 whole, which is shorter than its diff:
```python
import jax
import jax.numpy as jnp
from jax import lax
from jax.experimental import pallas as pl
from jax.experimental.pallas import tpu as pltpu
from jax.sharding import PartitionSpec as P

BF = jnp.bfloat16
F32 = jnp.float32
WIDE = 128
PAD = 136
BLOCK = 512
TOTALS = 4


def sigmoid(value):
    return 0.5 * jnp.tanh(0.5 * value) + 0.5


def pair_weights(kernel_ref, out_ref):
    depth = kernel_ref.shape[-1]
    zero = jnp.zeros((depth, depth), BF)
    for row in range(4):
        for col in range(3):
            at = (row * 3 + col) * depth
            out_ref[at : at + depth, :depth] = kernel_ref[row, col] if row < 3 else zero
            out_ref[at : at + depth, depth:] = kernel_ref[row - 1, col] if row > 0 else zero


def flipped_weights(kernel_ref, out_ref):
    depth = kernel_ref.shape[-1]
    zero = jnp.zeros((depth, depth), BF)
    for row in range(4):
        for col in range(3):
            at = (row * 3 + col) * depth
            out_ref[at : at + depth, :depth] = kernel_ref[2 - row, 2 - col].T if row < 3 else zero
            out_ref[at : at + depth, depth:] = kernel_ref[3 - row, 2 - col].T if row > 0 else zero


def clear_outside(ring):
    lat = lax.axis_index("lat")
    last = ring.shape[0] - 1
    ring[0, 0] = jnp.where(lat > 0, ring[0, 0], 0.0)
    ring[last, 1] = jnp.where(lat < lax.axis_size("lat") - 1, ring[last, 1], 0.0)


def taps_across(source_ref, taps_ref, start, width):
    depth = source_ref.shape[-1]
    for col in range(3):
        taps_ref[:, :, :, col * depth : (col + 1) * depth] = source_ref[
            :, :, start + col : start + col + width, :
        ].astype(BF)


def row_pairs(taps_ref, weights_ref, first, last):
    count, width, wide = last - first, taps_ref.shape[2], taps_ref.shape[3]
    rows = [
        taps_ref[first + a // 2 : last + a // 2, a % 2].reshape(count * width, wide)
        for a in range(4)
    ]
    total = jnp.dot(
        jnp.concatenate(rows, axis=1), weights_ref[...], preferred_element_type=F32
    )
    depth = wide // 3
    return (
        total[:, :depth].reshape(count, width, depth),
        total[:, depth:].reshape(count, width, depth),
    )


def spans(total, pieces):
    cuts = [total * i // pieces for i in range(pieces + 1)]
    return list(zip(cuts[:-1], cuts[1:]))


def pad_rim(padded_ref, top_ref, bottom_ref, left_ref, right_ref):
    pairs = padded_ref.shape[0]
    width = top_ref.shape[1]
    padded_ref[0, :, 8 : 8 + width, :] = top_ref[...].astype(F32)
    padded_ref[pairs - 1, :, 8 : 8 + width, :] = bottom_ref[...].astype(F32)
    padded_ref[:, :, 6:8, :] = left_ref[...].astype(F32).reshape(pairs, 2, 2, -1)
    padded_ref[:, :, 8 + width : 10 + width, :] = right_ref[...].astype(F32).reshape(
        pairs, 2, 2, -1
    )


def forward_kernel(
    cells_ref, top_ref, bottom_ref, left_ref, right_ref, bias_ref,
    x_hbm, first_hbm, second_hbm, into_hbm, out_hbm,
    predicted_hbm, z_slope_hbm, slope_hbm, second_back_hbm, first_back_hbm,
    padded, taps_one, hidden, taps_two, weights_one, weights_two, forecast, state,
    x_ref, first_ref, second_ref, into_ref, out_ref, sems,
    predicted_ref, z_slope_ref, slope_ref, second_back_ref, first_back_ref, out_sems,
):
    leaving = []

    def leave(source, into):
        leaving.append(pltpu.make_async_copy(source, into, out_sems.at[len(leaving)]))
        leaving[-1].start()

    sources = (x_hbm, first_hbm, second_hbm, into_hbm, out_hbm)
    fetched = (x_ref, first_ref, second_ref, into_ref, out_ref)
    copies = [
        pltpu.make_async_copy(source, into, sems.at[k])
        for k, (source, into) in enumerate(zip(sources, fetched))
    ]
    for copy in copies:
        copy.start()
    rows, width, depth = x_ref.shape
    for copy in copies:
        copy.wait()
    pair_weights(first_ref, weights_one)
    pair_weights(second_ref, weights_two)
    padded[1 : rows // 2 + 1, :, 8 : 8 + width, :] = (
        x_ref[...].astype(F32).reshape(rows // 2, 2, width, depth)
    )
    pad_rim(padded, top_ref, bottom_ref, left_ref, right_ref)
    taps_across(padded, taps_one, 6, WIDE)
    pairs = rows // 2 + 1
    for first, last in spans(pairs, 3):
        for odd, pre in enumerate(row_pairs(taps_one, weights_one, first, last)):
            sig = sigmoid(pre)
            hidden[first:last, odd] = pre * sig
            slope_ref[first:last, odd] = sig * (1.0 + pre * (1.0 - sig))
    leave(slope_ref, slope_hbm)
    clear_outside(hidden)
    taps_across(hidden, taps_two, 0, width)
    for first, last in spans(rows // 2, 4):
        for odd, change in enumerate(row_pairs(taps_two, weights_two, first, last)):
            for pair in range(first, last):
                row = 2 * pair + odd
                forecast[row * width : (row + 1) * width] = (
                    (x_ref[row].astype(F32) + change[pair - first]).astype(BF).astype(F32)
                )
    forecast[rows * width :] = jnp.zeros((forecast.shape[0] - rows * width, depth), F32)
    flipped_weights(second_ref, second_back_ref)
    flipped_weights(first_ref, first_back_ref)
    leave(second_back_ref, second_back_hbm)
    leave(first_back_ref, first_back_hbm)

    def take(slot, carry):
        state[pl.ds(slot, 1), :] = forecast[pl.ds(cells_ref[slot], 1), :]
        return carry

    taken = state.shape[0]
    lax.fori_loop(0, taken, take, 0, unroll=64)
    for first in range(0, taken, BLOCK):
        at = slice(first, first + BLOCK)
        z = jnp.dot(state[at].astype(BF), into_ref[...], preferred_element_type=F32)
        z = z + bias_ref[...]
        sig = sigmoid(z)
        z_slope_ref[at] = (sig * (1.0 + z * (1.0 - sig))).astype(BF)
        predicted_ref[at] = jnp.dot(
            (z * sig).astype(BF), out_ref[...], preferred_element_type=F32
        )
        leave(predicted_ref.at[at], predicted_hbm.at[at])
        leave(z_slope_ref.at[at], z_slope_hbm.at[at])
    for copy in leaving:
        copy.wait()


def scatter_kernel(
    cells_ref, out_t_ref, into_t_ref, radiance_hbm, predicted_hbm, z_slope_hbm,
    total_ref, head_ref, tail_ref, left_ref, right_ref,
    radiance, predicted, z_slope, sems, grads, *parts,
):
    taken = grads.shape[0]
    blocks = [slice(first, first + BLOCK) for first in range(0, taken, BLOCK)]
    copies = [
        [
            pltpu.make_async_copy(source.at[at], into.at[at], sems.at[k, j])
            for j, (source, into) in enumerate(
                ((radiance_hbm, radiance), (predicted_hbm, predicted), (z_slope_hbm, z_slope))
            )
        ]
        for k, at in enumerate(blocks)
    ]
    for group in copies:
        for copy in group:
            copy.start()
    for part in parts:
        part[...] = jnp.zeros(part.shape, F32)
    for at, group in zip(blocks, copies):
        for copy in group:
            copy.wait()
        misfit = (predicted[at] - radiance[at].astype(F32)).astype(BF)
        back = jnp.dot(misfit, out_t_ref[...], preferred_element_type=F32)
        grads[at] = jnp.dot(
            (back * z_slope[at].astype(F32)).astype(BF), into_t_ref[...], preferred_element_type=F32
        )

    def add(group, carry):
        slots = [group * len(parts) + k for k in range(len(parts))]
        ats = [pl.ds(cells_ref[slot], 1) for slot in slots]
        sums = [
            part[at, :] + grads[pl.ds(slot, 1), :] for part, at, slot in zip(parts, ats, slots)
        ]
        for part, at, value in zip(parts, ats, sums):
            part[at, :] = value
        return carry

    lax.fori_loop(0, taken // len(parts), add, 0, unroll=8)
    rows, width, depth = total_ref.shape
    total = parts[0][: rows * width]
    for part in parts[1:]:
        total = total + part[: rows * width]
    total = total.reshape(rows, width, depth)
    total_ref[...] = total
    head_ref[...] = total[:2].astype(BF)
    tail_ref[...] = total[rows - 2 :].astype(BF)
    left_ref[...] = total_ref[:, 0:2, :].astype(BF)
    right_ref[...] = total_ref[:, width - 2 : width, :].astype(BF)


def backward_kernel(
    d_ref, top_ref, bottom_ref, left_ref, right_ref, weights_one, weights_two, slope_ref,
    out_hbm,
    padded, taps_one, change, taps_two, out, sems,
):
    rows, width, depth = out.shape
    pairs = rows // 2 + 1
    padded[1:pairs, :, 8 : 8 + width] = d_ref[...].reshape(rows // 2, 2, width, depth)
    pad_rim(padded, top_ref, bottom_ref, left_ref, right_ref)
    taps_across(padded, taps_one, 6, WIDE)
    for first, last in spans(pairs, 3):
        for odd, dhidden in enumerate(row_pairs(taps_one, weights_one, first, last)):
            change[first:last, odd] = dhidden * slope_ref[first:last, odd]
    clear_outside(change)
    taps_across(change, taps_two, 0, width)
    leaving = []
    for k, (first, last) in enumerate(spans(rows // 2, 4)):
        for odd, back in enumerate(row_pairs(taps_two, weights_two, first, last)):
            for pair in range(first, last):
                out[2 * pair + odd] = d_ref[2 * pair + odd] + back[pair - first]
        at = slice(2 * first, 2 * last)
        leaving.append(pltpu.make_async_copy(out.at[at], out_hbm.at[at], sems.at[k]))
        leaving[-1].start()
    for copy in leaving:
        copy.wait()


VMEM = pl.BlockSpec(memory_space=pltpu.VMEM)
SMEM = pl.BlockSpec(memory_space=pltpu.SMEM)
HBM = pl.BlockSpec(memory_space=pltpu.HBM)


def params(mebibytes):
    return pltpu.CompilerParams(vmem_limit_bytes=mebibytes * 1024 * 1024)


def conv_scratch(rows, width, depth):
    return [
        pltpu.VMEM((rows // 2 + 2, 2, PAD, depth), F32),
        pltpu.VMEM((rows // 2 + 2, 2, WIDE, 3 * depth), BF),
        pltpu.VMEM((rows // 2 + 1, 2, WIDE, depth), F32),
        pltpu.VMEM((rows // 2 + 1, 2, width, 3 * depth), BF),
    ]


def swapped(array, axis, first, around):
    count = lax.axis_size(axis)
    pairs = [(i, (i + 1) % count) for i in range(first, count, 2) if around or i + 1 < count]
    return lax.ppermute(array, axis, [way for i, j in pairs for way in ((i, j), (j, i))])


def neighbours(low, high, axis, around):
    even = lax.rem(lax.axis_index(axis), 2) == 0
    one = swapped(jnp.where(even, high, low), axis, 0, around)
    two = swapped(jnp.where(even, low, high), axis, 1, around)
    return jnp.where(even, two, one), jnp.where(even, one, two)


def rows_around(head, tail):
    return neighbours(head, tail, "lat", False)


def columns_around(top, bottom, left, right):
    left = jnp.concatenate([top[:, :2], left, bottom[:, :2]], axis=0)
    right = jnp.concatenate([top[:, -2:], right, bottom[:, -2:]], axis=0)
    return neighbours(left, right, "lon", True)


def per_device(
    starting_vector, conv_first, later_stencil_matrix, obs_in, obs_bias, obs_out,
    innovations, counts, columns,
):
    rows, width, depth = starting_vector.shape
    lon_count, slots, channels = innovations.shape[1:]
    hidden_units = obs_in.shape[1]
    taken = lon_count * slots
    pairs = rows // 2 + 1

    live = lax.iota(jnp.int32, slots)[None, :] < counts[0][:, None]
    cells = jnp.where(live, columns[0], rows * width)
    cells = lax.all_to_all(cells, "lon", 0, 0, tiled=True).reshape(-1)
    x = starting_vector
    top, bottom = rows_around(x[:2], x[-2:])
    top, bottom, cells = lax.optimization_barrier((top, bottom, cells))
    ring = (top, bottom, *columns_around(top, bottom, x[:, :2], x[:, -2:]))
    ring, radiance = lax.optimization_barrier((ring, innovations[0]))
    radiance = lax.all_to_all(radiance, "lon", 0, 0, tiled=True).reshape(taken, channels)

    weights = jax.ShapeDtypeStruct((12 * depth, 2 * depth), BF)
    fetched = (x, conv_first, later_stencil_matrix, obs_in, obs_out)
    predicted, z_slope, slope, second_back, first_back = pl.pallas_call(
        forward_kernel,
        out_shape=(
            jax.ShapeDtypeStruct((taken, channels), F32),
            jax.ShapeDtypeStruct((taken, hidden_units), BF),
            jax.ShapeDtypeStruct((pairs, 2, WIDE, depth), F32),
            weights,
            weights,
        ),
        in_specs=[SMEM] + [VMEM] * 5 + [HBM] * 5,
        out_specs=(HBM,) * 5,
        scratch_shapes=conv_scratch(rows, width, depth)
        + [pltpu.VMEM((12 * depth, 2 * depth), BF)] * 2
        + [pltpu.VMEM((rows * width + 8, depth), F32), pltpu.VMEM((taken, depth), F32)]
        + [pltpu.VMEM(array.shape, array.dtype) for array in fetched]
        + [pltpu.SemaphoreType.DMA((len(fetched),))]
        + [
            pltpu.VMEM((taken, channels), F32),
            pltpu.VMEM((taken, hidden_units), BF),
            pltpu.VMEM((pairs, 2, WIDE, depth), F32),
            pltpu.VMEM(weights.shape, BF),
            pltpu.VMEM(weights.shape, BF),
            pltpu.SemaphoreType.DMA((3 + 2 * taken // BLOCK,)),
        ],
        compiler_params=params(60),
        name="forward",
    )(cells, *ring, obs_bias[None], *fetched)

    side = jax.ShapeDtypeStruct((rows, 2, depth), BF)
    edge = jax.ShapeDtypeStruct((2, width, depth), BF)
    dforecast, head, tail, left, right = pl.pallas_call(
        scatter_kernel,
        out_shape=(jax.ShapeDtypeStruct((rows, width, depth), F32), edge, edge, side, side),
        in_specs=[SMEM] + [VMEM] * 2 + [HBM] * 3,
        out_specs=(VMEM,) * 5,
        scratch_shapes=[
            pltpu.VMEM((taken, channels), BF),
            pltpu.VMEM((taken, channels), F32),
            pltpu.VMEM((taken, hidden_units), BF),
            pltpu.SemaphoreType.DMA((taken // BLOCK, 3)),
            pltpu.VMEM((taken, depth), F32),
        ]
        + [pltpu.VMEM((rows * width + 8, depth), F32)] * TOTALS,
        compiler_params=params(45),
        name="scatter",
    )(cells, obs_out.T, obs_in.T, radiance, predicted, z_slope)

    top, bottom = rows_around(head, tail)
    ring = (top, bottom, *columns_around(top, bottom, left, right))
    return pl.pallas_call(
        backward_kernel,
        out_shape=jax.ShapeDtypeStruct((rows, width, depth), F32),
        in_specs=[VMEM] * 8,
        out_specs=HBM,
        scratch_shapes=conv_scratch(rows, width, depth)
        + [pltpu.VMEM((rows, width, depth), F32), pltpu.SemaphoreType.DMA((4,))],
        compiler_params=params(34),
        name="backward",
    )(dforecast, *ring, second_back, first_back, slope)


def solution(mesh):
    placed = (
        P("lat", "lon", None),
        P(),
        P(),
        P(),
        P(),
        P(),
        P(("lat", "lon"), None, None, None),
        P(("lat", "lon"), None),
        P(("lat", "lon"), None, None),
    )
    return jax.shard_map(
        per_device, mesh=mesh, in_specs=placed, out_specs=P("lat", "lon", None), check_vma=False
    )
```

time: 144 us -> 106 us (0.74)
  blocking collectives: 16.7 us -> 0 us
  Pallas kernels: 56.7 us -> 42.4 us
  waiting for transfers between devices: 31.2 us -> 24.8 us
  local copies, waits for them, and re-layouts: 8.46 us -> 2.21 us
  starting transfers between devices: 27.3 us -> 32.1 us
    ppermute x8, waiting for transfers between devices: 31.2 us -> 14.4 us  [swapped(): lax.ppermute(array, axis, [way for i, j in pairs for way in ((i, j), (j,...]
    all_to_all x1 -> x0, blocking collectives: 16.7 us -> none  [per_device(): cells = lax.all_to_all(cells, 'lon', 0, 0, tiled=True).reshape(-1)]
    all_to_all x1 -> x2, starting transfers between devices: 4.01 us -> 16.3 us  [the longest x1 9.81 us: per_device(): cells = lax.all_to_all(cells, 'lon', 0, 0, tiled=True).reshape(-1)]
    all_to_all x1 -> x2, waiting for transfers between devices: 0.01 us -> 10.4 us  [the longest x1 10.4 us: per_device(): lax.all_to_all(radiance, 'lon', 0, 0, tiled=True).reshape(taken, channels)]
    pallas_call x3 -> x2, Pallas kernels: 43.6 us -> 33.7 us  [the longest x1 19.8 us: per_device(): pl.pallas_call(forward_kernel, out_shape=(jax.ShapeDtypeStruct((taken, ch...]
    ppermute x8, starting transfers between devices: 23.3 us -> 15.7 us  [swapped(): lax.ppermute(array, axis, [way for i, j in pairs for way in ((i, j), (j,...]
    pallas_call x1, Pallas kernels: 13.2 us -> 8.69 us  [per_device(): pl.pallas_call(backward_kernel, out_shape=jax.ShapeDtypeStruct((rows, wid...]
    unnamed x26 -> x22, local copies, waits for them, and re-layouts: 3.98 us -> 1.16 us
  transfers between devices with their start and end apart: 9 -> 10, of which waited for: 6 -> 6; matrix products, arithmetic and copies ran while one was open for 5% -> 2% of each run, Pallas kernels for 19% -> 19%
where the time goes in v1:
time: 106 us; the launch traced here: 105 us
  Pallas kernels  42.4 us (40%)
  starting transfers between devices  32.1 us (30%)
  waiting for transfers between devices  24.8 us (23%)
  other arithmetic  3.27 us (3%)
  local copies, waits for them, and re-layouts  2.21 us (2%)
    pallas_call x1, Pallas kernels, per_device(): pl.pallas_call(forward_kernel, out_shape=(jax.ShapeDtypeStruct((taken, ch...  19.8 us
    ppermute x8, starting transfers between devices, swapped(): lax.ppermute(array, axis, [way for i, j in pairs for way in ((i, j), (j,...  15.7 us
    ppermute x8, waiting for transfers between devices, swapped(): lax.ppermute(array, axis, [way for i, j in pairs for way in ((i, j), (j,...  14.4 us
    pallas_call x1, Pallas kernels, per_device(): pl.pallas_call(scatter_kernel, out_shape=(jax.ShapeDtypeStruct((rows, wid...  13.9 us
    all_to_all x1, waiting for transfers between devices, per_device(): lax.all_to_all(radiance, 'lon', 0, 0, tiled=True).reshape(taken, channels)  10.4 us
    all_to_all x1, starting transfers between devices, per_device(): cells = lax.all_to_all(cells, 'lon', 0, 0, tiled=True).reshape(-1)  9.81 us
    pallas_call x1, Pallas kernels, per_device(): pl.pallas_call(backward_kernel, out_shape=jax.ShapeDtypeStruct((rows, wid...  8.69 us
    all_to_all x1, starting transfers between devices, per_device(): lax.all_to_all(radiance, 'lon', 0, 0, tiled=True).reshape(taken, channels)  6.52 us
  transfers between devices with their start and end apart: 10, of which 6 were waited for; matrix products, arithmetic and copies ran while one was open for 2% of the time, Pallas kernels for 19%

profile of v1, /device:TPU:1, one launch (start us, length us, event | category | flops | bytes accessed | tf_op | source)
XLA Modules:
  0.0 105.2 jit_solution(10368609510027306514)
XLA Ops:
  0.0 0.0 copy-start.5
  0.0 0.0 copy-start.4
  0.0 1.5 %compare_select_fusion = s32[32,1,128]{2,1,0:T(1,128)} fusion(s32[32,1,128]{2,1,0:T(1,128)} %bitcast.32, s32[32]{0:T(128)} %bitcast.34), kind=kLoop, calls=%fused_computation.8 | loop fusion | flops 8192 | bytes 32896 | tf_op jit(solution)/shard_map/jit(_where)/select_n | solution.py:294
  1.5 9.8 %all-to-all-start = ((s32[32,1,128]{2,1,0:T(1,128)}), s32[32,1,128]{2,1,0:T(1,128)S(1)}, u32[]{:S(2)}, u32[]{:S(2)}) async-start(s32[32,1,128]{2,1,0:T(1,128)} %compare_select_fusion), calls=%async_computation | async-start | bytes 32768 | tf_op jit(solution)/shard_map/all_to_all | solution.py:295
  11.3 0.9 broadcast_select_fusion.14
  12.2 1.0 collective-permute-start.1
  13.2 4.3 %collective-permute-start = (bf16[2,112,128]{2,1,0:T(8,128)(2,1)S(1)}, bf16[2,112,128]{2,1,0:T(8,128)(2,1)S(1)}, u32[]{:S(2)}, u32[]{:S(2)}) collective-permute-start(bf16[2,112,128]{2,1,0:T(8,128)(2,1)S(1)} %get-tuple-element.44), channel_id=1, source_target_pairs={{32,64},{64,32},{33,65},{65,33},{34,66},{66,34},{35,67},{67,35},{3... | collective-permute-start | bytes 172040 | tf_op jit(solution)/shard_map/ppermute | solution.py:263
  17.5 1.0 fusion
  18.5 0.0 collective-permute-done.1
  18.5 1.7 %collective-permute-done = bf16[2,112,128]{2,1,0:T(8,128)(2,1)S(1)} collective-permute-done((bf16[2,112,128]{2,1,0:T(8,128)(2,1)S(1)}, bf16[2,112,128]{2,1,0:T(8,128)(2,1)S(1)}, u32[]{:S(2)}, u32[]{:S(2)}) %collective-permute-start) | collective-permute-done | bytes 57376 | tf_op jit(solution)/shard_map/ppermute | solution.py:263
  20.2 0.0 copy-start.6
  20.2 0.0 copy-start.7
  20.2 0.0 all-to-all-done
  20.2 0.0 copy-start.2
  20.3 0.1 broadcast_select_fusion.6
  20.4 1.6 %collective-permute-start.3 = (bf16[68,2,128]{2,1,0:T(2,128)(2,1)S(1)}, bf16[68,2,128]{2,1,0:T(2,128)(2,1)S(1)}, u32[]{:S(2)}, u32[]{:S(2)}) collective-permute-start(bf16[68,2,128]{2,1,0:T(2,128)(2,1)S(1)} %get-tuple-element.57), channel_id=1, source_target_pairs={{0,1},{1,0},{2,3},{3,2},{4,5},{5,4},{6,7},{7,6},{8,9},{9,8},{10,11... | collective-permute-start | bytes 104456 | tf_op jit(solution)/shard_map/ppermute | solution.py:263
  22.0 5.0 %collective-permute-start.2 = (bf16[68,2,128]{2,1,0:T(2,128)(2,1)S(1)}, bf16[68,2,128]{2,1,0:T(2,128)(2,1)S(1)}, u32[]{:S(2)}, u32[]{:S(2)}) collective-permute-start(bf16[68,2,128]{2,1,0:T(2,128)(2,1)S(1)} %get-tuple-element.58), channel_id=1, source_target_pairs={{1,2},{2,1},{3,4},{4,3},{5,6},{6,5},{7,8},{8,7},{9,10},{10,9},{11,... | collective-permute-start | bytes 104456 | tf_op jit(solution)/shard_map/ppermute | solution.py:263
  27.0 0.0 collective-permute-done.3
  27.0 2.1 %collective-permute-done.2 = bf16[68,2,128]{2,1,0:T(2,128)(2,1)S(1)} collective-permute-done((bf16[68,2,128]{2,1,0:T(2,128)(2,1)S(1)}, bf16[68,2,128]{2,1,0:T(2,128)(2,1)S(1)}, u32[]{:S(2)}, u32[]{:S(2)}) %collective-permute-start.2) | collective-permute-done | bytes 34848 | tf_op jit(solution)/shard_map/ppermute | solution.py:263
  29.1 0.6 broadcast_select_fusion.4
  29.8 6.5 %all-to-all-start.1 = ((bf16[32,128,256]{2,1,0:T(8,128)(2,1)}), bf16[32,128,256]{2,1,0:T(8,128)(2,1)S(1)}, u32[]{:S(2)}, u32[]{:S(2)}) async-start(bf16[32,128,256]{2,1,0:T(8,128)(2,1)} %bitcast.25), calls=%async_computation.1 | async-start | bytes 4194304 | tf_op jit(solution)/shard_map/all_to_all | solution.py:301
  36.3 0.0 copy-done.5
  36.3 0.1 copy.13
  36.4 0.0 copy-done.4
  36.4 0.1 copy.12
  36.6 0.0 copy-done.6
  36.6 0.0 copy-done.7
  36.6 0.0 copy-done.2
  36.6 19.8 %forward.1 = (f32[4096,256]{1,0:T(8,128)}, bf16[4096,512]{1,0:T(8,128)(2,1)}, f32[33,2,128,128]{3,2,1,0:T(8,128)}, bf16[1536,256]{1,0:T(8,128)(2,1)}, bf16[1536,256]{1,0:T(8,128)(2,1)}) custom-call(s32[4096]{0:T(1024)} %bitcast.21, bf16[2,112,128]{2,1,0:T(8,128)(2,1)} %copy-done.7, bf16[2,112,128]{2,1,0:T(8,128)(2,1)} %copy-done.6, ...), custom_call_target="tpu_custom_call" | custom-call | tf_op jit(solution)/shard_map/forward/pallas_call | solution.py:305
  56.4 10.4 %all-to-all-done.1 = bf16[32,128,256]{2,1,0:T(8,128)(2,1)S(1)} async-done(((bf16[32,128,256]{2,1,0:T(8,128)(2,1)}), bf16[32,128,256]{2,1,0:T(8,128)(2,1)S(1)}, u32[]{:S(2)}, u32[]{:S(2)}) %all-to-all-start.1) | async-done | bytes 2097184 | tf_op jit(solution)/shard_map/all_to_all | solution.py:301
  66.8 0.0 slice-start
  66.8 0.0 copy-start.3
  66.8 0.9 copy-done.3
  67.7 13.9 %scatter.1 = (f32[64,112,128]{2,1,0:T(8,128)S(1)}, bf16[2,112,128]{2,1,0:T(8,128)(2,1)S(1)}, bf16[2,112,128]{2,1,0:T(8,128)(2,1)S(1)}, bf16[64,2,128]{2,1,0:T(2,128)(2,1)S(1)}, bf16[64,2,128]{2,1,0:T(2,128)(2,1)S(1)}) custom-call(s32[4096]{0:T(1024)S(1)} %bitcast.22, bf16[256,512]{1,0:T(8,128)(2,1)S(1)} %bitcast.19, bf16[512,128]{1,0:T(8,128)(2,1)S(1)} %bitcast.20, ...), custom_call_target="tpu_custom_call" | custom-call | tf_op jit(solution)/shard_map/scatter/pallas_call | solution.py:335
  81.6 0.1 collective-permute-start.5
  81.7 1.9 %collective-permute-start.4 = (bf16[2,112,128]{2,1,0:T(8,128)(2,1)S(1)}, bf16[2,112,128]{2,1,0:T(8,128)(2,1)S(1)}, u32[]{:S(2)}, u32[]{:S(2)}) collective-permute-start(bf16[2,112,128]{2,1,0:T(8,128)(2,1)S(1)} %get-tuple-element.48), channel_id=1, source_target_pairs={{32,64},{64,32},{33,65},{65,33},{34,66},{66,34},{35,67},{67,35},{3... | collective-permute-start | bytes 172040 | tf_op jit(solution)/shard_map/ppermute | solution.py:263
  83.6 0.0 collective-permute-done.5
  83.6 5.1 %collective-permute-done.4 = bf16[2,112,128]{2,1,0:T(8,128)(2,1)S(1)} collective-permute-done((bf16[2,112,128]{2,1,0:T(8,128)(2,1)S(1)}, bf16[2,112,128]{2,1,0:T(8,128)(2,1)S(1)}, u32[]{:S(2)}, u32[]{:S(2)}) %collective-permute-start.4) | collective-permute-done | bytes 57376 | tf_op jit(solution)/shard_map/ppermute | solution.py:263
  88.7 0.1 broadcast_select_fusion.2
  88.9 0.1 collective-permute-start.7
  89.0 1.8 %collective-permute-start.6 = (bf16[68,2,128]{2,1,0:T(2,128)(2,1)S(1)}, bf16[68,2,128]{2,1,0:T(2,128)(2,1)S(1)}, u32[]{:S(2)}, u32[]{:S(2)}) collective-permute-start(bf16[68,2,128]{2,1,0:T(2,128)(2,1)S(1)} %get-tuple-element.54), channel_id=1, source_target_pairs={{1,2},{2,1},{3,4},{4,3},{5,6},{6,5},{7,8},{8,7},{9,10},{10,9},{11,... | collective-permute-start | bytes 104456 | tf_op jit(solution)/shard_map/ppermute | solution.py:263
  90.7 1.0 collective-permute-done.7
  91.7 4.5 %collective-permute-done.6 = bf16[68,2,128]{2,1,0:T(2,128)(2,1)S(1)} collective-permute-done((bf16[68,2,128]{2,1,0:T(2,128)(2,1)S(1)}, bf16[68,2,128]{2,1,0:T(2,128)(2,1)S(1)}, u32[]{:S(2)}, u32[]{:S(2)}) %collective-permute-start.6) | collective-permute-done | bytes 34848 | tf_op jit(solution)/shard_map/ppermute | solution.py:263
  96.3 0.0 slice-done
  96.3 0.0 slice-done.1
  96.3 0.0 copy-done
  96.3 0.0 copy-done.1
  96.3 8.7 %backward.1 = f32[64,112,128]{2,1,0:T(8,128)} custom-call(f32[64,112,128]{2,1,0:T(8,128)S(1)} %get-tuple-element.33.d_ref, bf16[2,112,128]{2,1,0:T(8,128)(2,1)S(1)} %get-tuple-element.46.top_ref, bf16[2,112,128]{2,1,0:T(8,128)(2,1)S(1)} %get-tuple-element.45.bottom_ref, bf16[68,2,128]{2,1,0:T(2,128)(2,1)S(1)} %bitcast.24, bf16[68,2,128]{2,1,0:T(2,128)(2,1)S(1)} %bitcast.23, ...), custom_call_target="tpu_custom_call" | custom-call | tf_op jit(solution)/shard_map/backward/pallas_call | solution.py:354
  (11 shorter events, 0.1 us)
Async XLA Ops:
  0.0 36.3 %copy-start.5 = (bf16[128,512]{1,0:T(8,128)(2,1)S(1)}, bf16[128,512]{1,0:T(8,128)(2,1)}, u32[]{:S(2)}) copy-start(bf16[128,512]{1,0:T(8,128)(2,1)} %into_hbm.1) | copy-start | bytes 393220
  0.0 36.4 %copy-start.4 = (bf16[512,256]{1,0:T(8,128)(2,1)S(1)}, bf16[512,256]{1,0:T(8,128)(2,1)}, u32[]{:S(2)}) copy-start(bf16[512,256]{1,0:T(8,128)(2,1)} %out_hbm.1) | copy-start | bytes 786436
  1.5 18.8 %all-to-all-start = ((s32[32,1,128]{2,1,0:T(1,128)}), s32[32,1,128]{2,1,0:T(1,128)S(1)}, u32[]{:S(2)}, u32[]{:S(2)}) async-start(s32[32,1,128]{2,1,0:T(1,128)} %compare_select_fusion), calls=%async_computation | async-start | bytes 32768 | tf_op jit(solution)/shard_map/all_to_all | solution.py:295
  12.2 6.3 %collective-permute-start.1 = (bf16[2,112,128]{2,1,0:T(8,128)(2,1)S(1)}, bf16[2,112,128]{2,1,0:T(8,128)(2,1)S(1)}, u32[]{:S(2)}, u32[]{:S(2)}) collective-permute-start(bf16[2,112,128]{2,1,0:T(8,128)(2,1)S(1)} %get-tuple-element.43), channel_id=1, source_target_pairs={{0,32},{32,0},{64,96},{96,64},{1,33},{33,1},{65,97},{97,65},{2,34}... | collective-permute-start | bytes 172040 | tf_op jit(solution)/shard_map/ppermute | solution.py:263
  13.2 7.0 %collective-permute-start = (bf16[2,112,128]{2,1,0:T(8,128)(2,1)S(1)}, bf16[2,112,128]{2,1,0:T(8,128)(2,1)S(1)}, u32[]{:S(2)}, u32[]{:S(2)}) collective-permute-start(bf16[2,112,128]{2,1,0:T(8,128)(2,1)S(1)} %get-tuple-element.44), channel_id=1, source_target_pairs={{32,64},{64,32},{33,65},{65,33},{34,66},{66,34},{35,67},{67,35},{3... | collective-permute-start | bytes 172040 | tf_op jit(solution)/shard_map/ppermute | solution.py:263
  20.2 16.4 %copy-start.6 = (bf16[2,112,128]{2,1,0:T(8,128)(2,1)}, bf16[2,112,128]{2,1,0:T(8,128)(2,1)S(1)}, u32[]{:S(2)}) copy-start(bf16[2,112,128]{2,1,0:T(8,128)(2,1)S(1)} %get-tuple-element.28.bottom_ref) | copy-start | bytes 172036
  20.2 16.4 %copy-start.7 = (bf16[2,112,128]{2,1,0:T(8,128)(2,1)}, bf16[2,112,128]{2,1,0:T(8,128)(2,1)S(1)}, u32[]{:S(2)}) copy-start(bf16[2,112,128]{2,1,0:T(8,128)(2,1)S(1)} %get-tuple-element.27.top_ref) | copy-start | bytes 172036
  20.2 16.4 %copy-start.2 = (s32[32,1,128]{2,1,0:T(1,128)}, s32[32,1,128]{2,1,0:T(1,128)S(1)}, u32[]{:S(2)}) copy-start(s32[32,1,128]{2,1,0:T(1,128)S(1)} %all-to-all-done) | copy-start | bytes 49156
  20.4 6.6 %collective-permute-start.3 = (bf16[68,2,128]{2,1,0:T(2,128)(2,1)S(1)}, bf16[68,2,128]{2,1,0:T(2,128)(2,1)S(1)}, u32[]{:S(2)}, u32[]{:S(2)}) collective-permute-start(bf16[68,2,128]{2,1,0:T(2,128)(2,1)S(1)} %get-tuple-element.57), channel_id=1, source_target_pairs={{0,1},{1,0},{2,3},{3,2},{4,5},{5,4},{6,7},{7,6},{8,9},{9,8},{10,11... | collective-permute-start | bytes 104456 | tf_op jit(solution)/shard_map/ppermute | solution.py:263
  22.0 7.1 %collective-permute-start.2 = (bf16[68,2,128]{2,1,0:T(2,128)(2,1)S(1)}, bf16[68,2,128]{2,1,0:T(2,128)(2,1)S(1)}, u32[]{:S(2)}, u32[]{:S(2)}) collective-permute-start(bf16[68,2,128]{2,1,0:T(2,128)(2,1)S(1)} %get-tuple-element.58), channel_id=1, source_target_pairs={{1,2},{2,1},{3,4},{4,3},{5,6},{6,5},{7,8},{8,7},{9,10},{10,9},{11,... | collective-permute-start | bytes 104456 | tf_op jit(solution)/shard_map/ppermute | solution.py:263
  29.8 37.0 %all-to-all-start.1 = ((bf16[32,128,256]{2,1,0:T(8,128)(2,1)}), bf16[32,128,256]{2,1,0:T(8,128)(2,1)S(1)}, u32[]{:S(2)}, u32[]{:S(2)}) async-start(bf16[32,128,256]{2,1,0:T(8,128)(2,1)} %bitcast.25), calls=%async_computation.1 | async-start | bytes 4194304 | tf_op jit(solution)/shard_map/all_to_all | solution.py:301
  66.8 29.5 %slice-start = ((s8[4325376]{0:T(1024)(128)(4,1)}), s8[4194304]{0:T(1024)(128)(4,1)S(1)}, s32[]{:S(2)}) async-start(s8[4325376]{0:T(1024)(128)(4,1)} %bitcast.17), calls=%async_computation.2 | async-start | bytes 8388608
  66.8 0.9 copy-start.3
  67.7 28.6 %slice-start.1 = ((s8[4325376]{0:T(1024)(128)(4,1)}), s8[131072]{0:T(1024)(128)(4,1)S(1)}, s32[]{:S(2)}) async-start(s8[4325376]{0:T(1024)(128)(4,1)} %bitcast.17), calls=%async_computation.3 | async-start | bytes 262144
  67.7 28.6 %copy-start = (bf16[1536,256]{1,0:T(8,128)(2,1)S(1)}, bf16[1536,256]{1,0:T(8,128)(2,1)}, u32[]{:S(2)}) copy-start(bf16[1536,256]{1,0:T(8,128)(2,1)} %get-tuple-element.38.weights_one) | copy-start | bytes 2359300
  67.7 28.7 %copy-start.1 = (bf16[1536,256]{1,0:T(8,128)(2,1)S(1)}, bf16[1536,256]{1,0:T(8,128)(2,1)}, u32[]{:S(2)}) copy-start(bf16[1536,256]{1,0:T(8,128)(2,1)} %get-tuple-element.39.weights_two) | copy-start | bytes 2359300
  81.6 2.0 %collective-permute-start.5 = (bf16[2,112,128]{2,1,0:T(8,128)(2,1)S(1)}, bf16[2,112,128]{2,1,0:T(8,128)(2,1)S(1)}, u32[]{:S(2)}, u32[]{:S(2)}) collective-permute-start(bf16[2,112,128]{2,1,0:T(8,128)(2,1)S(1)} %get-tuple-element.47), channel_id=1, source_target_pairs={{0,32},{32,0},{64,96},{96,64},{1,33},{33,1},{65,97},{97,65},{2,34}... | collective-permute-start | bytes 172040 | tf_op jit(solution)/shard_map/ppermute | solution.py:263
  81.7 7.0 %collective-permute-start.4 = (bf16[2,112,128]{2,1,0:T(8,128)(2,1)S(1)}, bf16[2,112,128]{2,1,0:T(8,128)(2,1)S(1)}, u32[]{:S(2)}, u32[]{:S(2)}) collective-permute-start(bf16[2,112,128]{2,1,0:T(8,128)(2,1)S(1)} %get-tuple-element.48), channel_id=1, source_target_pairs={{32,64},{64,32},{33,65},{65,33},{34,66},{66,34},{35,67},{67,35},{3... | collective-permute-start | bytes 172040 | tf_op jit(solution)/shard_map/ppermute | solution.py:263
  88.9 2.9 %collective-permute-start.7 = (bf16[68,2,128]{2,1,0:T(2,128)(2,1)S(1)}, bf16[68,2,128]{2,1,0:T(2,128)(2,1)S(1)}, u32[]{:S(2)}, u32[]{:S(2)}) collective-permute-start(bf16[68,2,128]{2,1,0:T(2,128)(2,1)S(1)} %get-tuple-element.53), channel_id=1, source_target_pairs={{0,1},{1,0},{2,3},{3,2},{4,5},{5,4},{6,7},{7,6},{8,9},{9,8},{10,11... | collective-permute-start | bytes 104456 | tf_op jit(solution)/shard_map/ppermute | solution.py:263
  89.0 7.3 %collective-permute-start.6 = (bf16[68,2,128]{2,1,0:T(2,128)(2,1)S(1)}, bf16[68,2,128]{2,1,0:T(2,128)(2,1)S(1)}, u32[]{:S(2)}, u32[]{:S(2)}) collective-permute-start(bf16[68,2,128]{2,1,0:T(2,128)(2,1)S(1)} %get-tuple-element.54), channel_id=1, source_target_pairs={{1,2},{2,1},{3,4},{4,3},{5,6},{6,5},{7,8},{8,7},{9,10},{10,9},{11,... | collective-permute-start | bytes 104456 | tf_op jit(solution)/shard_map/ppermute | solution.py:263

commit v2 on v1

--- a/solution.py
+++ b/solution.py
@@ -10,6 +10,7 @@
 WIDE = 128
 PAD = 136
 BLOCK = 512
+GROUP = 1024
 TOTALS = 4
 
 
@@ -44,11 +45,12 @@
     ring[last, 1] = jnp.where(lat < lax.axis_size("lat") - 1, ring[last, 1], 0.0)
 
 
-def taps_across(source_ref, taps_ref, start, width):
+def taps_across(source_ref, taps_ref, start, width, first=0, last=None):
     depth = source_ref.shape[-1]
+    of = slice(first, source_ref.shape[0] if last is None else last)
     for col in range(3):
-        taps_ref[:, :, :, col * depth : (col + 1) * depth] = source_ref[
-            :, :, start + col : start + col + width, :
+        taps_ref[of, :, :, col * depth : (col + 1) * depth] = source_ref[
+            of, :, start + col : start + col + width, :
         ].astype(BF)
 
 
@@ -87,7 +89,7 @@
 def forward_kernel(
     cells_ref, top_ref, bottom_ref, left_ref, right_ref, bias_ref,
     x_hbm, first_hbm, second_hbm, into_hbm, out_hbm,
-    predicted_hbm, z_slope_hbm, slope_hbm, second_back_hbm, first_back_hbm,
+    predicted_hbm, z_slope_hbm, slope_hbm, second_back_hbm, first_back_hbm, cells_hbm,
     padded, taps_one, hidden, taps_two, weights_one, weights_two, forecast, state,
     x_ref, first_ref, second_ref, into_ref, out_ref, sems,
     predicted_ref, z_slope_ref, slope_ref, second_back_ref, first_back_ref, out_sems,
@@ -135,6 +137,7 @@
     forecast[rows * width :] = jnp.zeros((forecast.shape[0] - rows * width, depth), F32)
     flipped_weights(second_ref, second_back_ref)
     flipped_weights(first_ref, first_back_ref)
+    leave(cells_ref, cells_hbm.at[pl.ds(0, cells_ref.shape[0])])
     leave(second_back_ref, second_back_hbm)
     leave(first_back_ref, first_back_hbm)
 
@@ -160,17 +163,19 @@
 
 
 def scatter_kernel(
-    cells_ref, out_t_ref, into_t_ref, radiance_hbm, predicted_hbm, z_slope_hbm,
+    out_t_ref, into_t_ref, radiance_ref, predicted_hbm, z_slope_hbm, cells_hbm,
     total_ref, head_ref, tail_ref, left_ref, right_ref,
-    radiance, predicted, z_slope, sems, grads, *parts,
+    predicted, z_slope, sems, cells_ref, cells_sem, grads, *parts,
 ):
     taken = grads.shape[0]
-    blocks = [slice(first, first + BLOCK) for first in range(0, taken, BLOCK)]
+    cells_copy = pltpu.make_async_copy(cells_hbm.at[pl.ds(0, taken)], cells_ref, cells_sem)
+    cells_copy.start()
+    blocks = [slice(first, first + GROUP) for first in range(0, taken, GROUP)]
     copies = [
         [
             pltpu.make_async_copy(source.at[at], into.at[at], sems.at[k, j])
             for j, (source, into) in enumerate(
-                ((radiance_hbm, radiance), (predicted_hbm, predicted), (z_slope_hbm, z_slope))
+                ((predicted_hbm, predicted), (z_slope_hbm, z_slope))
             )
         ]
         for k, at in enumerate(blocks)
@@ -180,14 +185,7 @@
             copy.start()
     for part in parts:
         part[...] = jnp.zeros(part.shape, F32)
-    for at, group in zip(blocks, copies):
-        for copy in group:
-            copy.wait()
-        misfit = (predicted[at] - radiance[at].astype(F32)).astype(BF)
-        back = jnp.dot(misfit, out_t_ref[...], preferred_element_type=F32)
-        grads[at] = jnp.dot(
-            (back * z_slope[at].astype(F32)).astype(BF), into_t_ref[...], preferred_element_type=F32
-        )
+    cells_copy.wait()
 
     def add(group, carry):
         slots = [group * len(parts) + k for k in range(len(parts))]
@@ -199,7 +197,17 @@
             part[at, :] = value
         return carry
 
-    lax.fori_loop(0, taken // len(parts), add, 0, unroll=8)
+    for at, group in zip(blocks, copies):
+        for copy in group:
+            copy.wait()
+        misfit = (predicted[at] - radiance_ref[at].astype(F32)).astype(BF)
+        back = jnp.dot(misfit, out_t_ref[...], preferred_element_type=F32)
+        grads[at] = jnp.dot(
+            (back * z_slope[at].astype(F32)).astype(BF),
+            into_t_ref[...],
+            preferred_element_type=F32,
+        )
+        lax.fori_loop(at.start // len(parts), at.stop // len(parts), add, 0, unroll=8)
     rows, width, depth = total_ref.shape
     total = parts[0][: rows * width]
     for part in parts[1:]:
@@ -219,16 +227,23 @@
 ):
     rows, width, depth = out.shape
     pairs = rows // 2 + 1
-    padded[1:pairs, :, 8 : 8 + width] = d_ref[...].reshape(rows // 2, 2, width, depth)
     pad_rim(padded, top_ref, bottom_ref, left_ref, right_ref)
-    taps_across(padded, taps_one, 6, WIDE)
-    for first, last in spans(pairs, 3):
+    made = 0
+    for first, last in spans(pairs, 6):
+        low, high = max(made, 1), min(last + 1, pairs)
+        padded[low:high, :, 8 : 8 + width] = d_ref[2 * low - 2 : 2 * high - 2].reshape(
+            high - low, 2, width, depth
+        )
+        taps_across(padded, taps_one, 6, WIDE, made, last + 1)
+        made = last + 1
         for odd, dhidden in enumerate(row_pairs(taps_one, weights_one, first, last)):
             change[first:last, odd] = dhidden * slope_ref[first:last, odd]
     clear_outside(change)
-    taps_across(change, taps_two, 0, width)
+    made = 0
     leaving = []
-    for k, (first, last) in enumerate(spans(rows // 2, 4)):
+    for k, (first, last) in enumerate(spans(rows // 2, 8)):
+        taps_across(change, taps_two, 0, width, made, last + 1)
+        made = last + 1
         for odd, back in enumerate(row_pairs(taps_two, weights_two, first, last)):
             for pair in range(first, last):
                 out[2 * pair + odd] = d_ref[2 * pair + odd] + back[pair - first]
@@ -263,21 +278,22 @@
     return lax.ppermute(array, axis, [way for i, j in pairs for way in ((i, j), (j, i))])
 
 
-def neighbours(low, high, axis, around):
+def neighbours(low, high, axis, around, after=()):
     even = lax.rem(lax.axis_index(axis), 2) == 0
     one = swapped(jnp.where(even, high, low), axis, 0, around)
     two = swapped(jnp.where(even, low, high), axis, 1, around)
-    return jnp.where(even, two, one), jnp.where(even, one, two)
+    one, two, after = lax.optimization_barrier((one, two, after))
+    return (jnp.where(even, two, one), jnp.where(even, one, two)), after
 
 
 def rows_around(head, tail):
-    return neighbours(head, tail, "lat", False)
-
-
-def columns_around(top, bottom, left, right):
+    return neighbours(head, tail, "lat", False)[0]
+
+
+def columns_around(top, bottom, left, right, after=()):
     left = jnp.concatenate([top[:, :2], left, bottom[:, :2]], axis=0)
     right = jnp.concatenate([top[:, -2:], right, bottom[:, -2:]], axis=0)
-    return neighbours(left, right, "lon", True)
+    return neighbours(left, right, "lon", True, after)
 
 
 def per_device(
@@ -296,13 +312,13 @@
     x = starting_vector
     top, bottom = rows_around(x[:2], x[-2:])
     top, bottom, cells = lax.optimization_barrier((top, bottom, cells))
-    ring = (top, bottom, *columns_around(top, bottom, x[:, :2], x[:, -2:]))
-    ring, radiance = lax.optimization_barrier((ring, innovations[0]))
+    sides, radiance = columns_around(top, bottom, x[:, :2], x[:, -2:], innovations[0])
+    ring = (top, bottom, *sides)
     radiance = lax.all_to_all(radiance, "lon", 0, 0, tiled=True).reshape(taken, channels)
 
     weights = jax.ShapeDtypeStruct((12 * depth, 2 * depth), BF)
     fetched = (x, conv_first, later_stencil_matrix, obs_in, obs_out)
-    predicted, z_slope, slope, second_back, first_back = pl.pallas_call(
+    predicted, z_slope, slope, second_back, first_back, cells = pl.pallas_call(
         forward_kernel,
         out_shape=(
             jax.ShapeDtypeStruct((taken, channels), F32),
@@ -310,9 +326,10 @@
             jax.ShapeDtypeStruct((pairs, 2, WIDE, depth), F32),
             weights,
             weights,
+            jax.ShapeDtypeStruct((taken * 1024,), jnp.int32),
         ),
         in_specs=[SMEM] + [VMEM] * 5 + [HBM] * 5,
-        out_specs=(HBM,) * 5,
+        out_specs=(HBM,) * 6,
         scratch_shapes=conv_scratch(rows, width, depth)
         + [pltpu.VMEM((12 * depth, 2 * depth), BF)] * 2
         + [pltpu.VMEM((rows * width + 8, depth), F32), pltpu.VMEM((taken, depth), F32)]
@@ -324,7 +341,7 @@
             pltpu.VMEM((pairs, 2, WIDE, depth), F32),
             pltpu.VMEM(weights.shape, BF),
             pltpu.VMEM(weights.shape, BF),
-            pltpu.SemaphoreType.DMA((3 + 2 * taken // BLOCK,)),
+            pltpu.SemaphoreType.DMA((4 + 2 * taken // BLOCK,)),
         ],
         compiler_params=params(60),
         name="forward",
@@ -335,29 +352,30 @@
     dforecast, head, tail, left, right = pl.pallas_call(
         scatter_kernel,
         out_shape=(jax.ShapeDtypeStruct((rows, width, depth), F32), edge, edge, side, side),
-        in_specs=[SMEM] + [VMEM] * 2 + [HBM] * 3,
+        in_specs=[VMEM] * 3 + [HBM] * 3,
         out_specs=(VMEM,) * 5,
         scratch_shapes=[
-            pltpu.VMEM((taken, channels), BF),
             pltpu.VMEM((taken, channels), F32),
             pltpu.VMEM((taken, hidden_units), BF),
-            pltpu.SemaphoreType.DMA((taken // BLOCK, 3)),
+            pltpu.SemaphoreType.DMA((taken // GROUP, 2)),
+            pltpu.SMEM((taken,), jnp.int32),
+            pltpu.SemaphoreType.DMA(()),
             pltpu.VMEM((taken, depth), F32),
         ]
         + [pltpu.VMEM((rows * width + 8, depth), F32)] * TOTALS,
         compiler_params=params(45),
         name="scatter",
-    )(cells, obs_out.T, obs_in.T, radiance, predicted, z_slope)
+    )(obs_out.T, obs_in.T, radiance, predicted, z_slope, cells)
 
     top, bottom = rows_around(head, tail)
-    ring = (top, bottom, *columns_around(top, bottom, left, right))
+    ring = (top, bottom, *columns_around(top, bottom, left, right)[0])
     return pl.pallas_call(
         backward_kernel,
         out_shape=jax.ShapeDtypeStruct((rows, width, depth), F32),
         in_specs=[VMEM] * 8,
         out_specs=HBM,
         scratch_shapes=conv_scratch(rows, width, depth)
-        + [pltpu.VMEM((rows, width, depth), F32), pltpu.SemaphoreType.DMA((4,))],
+        + [pltpu.VMEM((rows, width, depth), F32), pltpu.SemaphoreType.DMA((8,))],
         compiler_params=params(34),
         name="backward",
     )(dforecast, *ring, second_back, first_back, slope)

time: 106 us -> 101 us (0.953)
  starting transfers between devices: 32.1 us -> 29.5 us
  Pallas kernels: 42.4 us -> 40.5 us
    ppermute x8, starting transfers between devices: 15.7 us -> 13.5 us  [swapped(): lax.ppermute(array, axis, [way for i, j in pairs for way in ((i, j), (j,...]
    pallas_call x1, Pallas kernels: 13.9 us -> 12.1 us  [per_device(): pl.pallas_call(scatter_kernel, out_shape=(jax.ShapeDtypeStruct((rows, wid...]
  transfers between devices with their start and end apart: 10 -> 10, of which waited for: 6 -> 6; matrix products, arithmetic and copies ran while one was open for 2% -> 3% of each run, Pallas kernels for 19% -> 20%
where the time goes in v2:
time: 101 us
  Pallas kernels  40.5 us (40%)
  starting transfers between devices  29.5 us (29%)
  waiting for transfers between devices  25.5 us (25%)
  other arithmetic  3.3 us (3%)
  local copies, waits for them, and re-layouts  1.34 us (1%)
    pallas_call x1, Pallas kernels, per_device(): pl.pallas_call(forward_kernel, out_shape=(jax.ShapeDtypeStruct((taken, ch...  19.9 us
    ppermute x8, waiting for transfers between devices, swapped(): lax.ppermute(array, axis, [way for i, j in pairs for way in ((i, j), (j,...  15.3 us
    ppermute x8, starting transfers between devices, swapped(): lax.ppermute(array, axis, [way for i, j in pairs for way in ((i, j), (j,...  13.5 us
    pallas_call x1, Pallas kernels, per_device(): pl.pallas_call(scatter_kernel, out_shape=(jax.ShapeDtypeStruct((rows, wid...  12.1 us
    all_to_all x1, waiting for transfers between devices, per_device(): lax.all_to_all(radiance, 'lon', 0, 0, tiled=True).reshape(taken, channels)  10.2 us
    all_to_all x1, starting transfers between devices, per_device(): cells = lax.all_to_all(cells, 'lon', 0, 0, tiled=True).reshape(-1)  9.81 us
    pallas_call x1, Pallas kernels, per_device(): pl.pallas_call(backward_kernel, out_shape=jax.ShapeDtypeStruct((rows, wid...  8.45 us
    all_to_all x1, starting transfers between devices, per_device(): lax.all_to_all(radiance, 'lon', 0, 0, tiled=True).reshape(taken, channels)  6.13 us
  transfers between devices with their start and end apart: 10, of which 6 were waited for; matrix products, arithmetic and copies ran while one was open for 3% of the time, Pallas kernels for 20%

profile of v2, /device:TPU:1, one launch (start us, length us, event | category | flops | bytes accessed | tf_op | source)
XLA Modules:
  0.0 100.6 jit_solution(2250224462746081217)
XLA Ops:
  0.0 0.0 copy-start.3
  0.0 0.0 copy-start.2
  0.0 1.5 %compare_select_fusion = s32[32,1,128]{2,1,0:T(1,128)} fusion(s32[32,1,128]{2,1,0:T(1,128)} %bitcast.31, s32[32]{0:T(128)} %bitcast.33), kind=kLoop, calls=%fused_computation.8 | loop fusion | flops 8192 | bytes 32896 | tf_op jit(solution)/shard_map/jit(_where)/select_n | solution.py:310
  1.5 9.8 %all-to-all-start = ((s32[32,1,128]{2,1,0:T(1,128)}), s32[32,1,128]{2,1,0:T(1,128)S(1)}, u32[]{:S(2)}, u32[]{:S(2)}) async-start(s32[32,1,128]{2,1,0:T(1,128)} %compare_select_fusion), calls=%async_computation | async-start | bytes 32768 | tf_op jit(solution)/shard_map/all_to_all | solution.py:311
  11.3 0.9 broadcast_select_fusion.14
  12.2 5.2 %collective-permute-start.1 = (bf16[2,112,128]{2,1,0:T(8,128)(2,1)S(1)}, bf16[2,112,128]{2,1,0:T(8,128)(2,1)S(1)}, u32[]{:S(2)}, u32[]{:S(2)}) collective-permute-start(bf16[2,112,128]{2,1,0:T(8,128)(2,1)S(1)} %get-tuple-element.53), channel_id=1, source_target_pairs={{32,64},{64,32},{33,65},{65,33},{34,66},{66,34},{35,67},{67,35},{3... | collective-permute-start | bytes 172040 | tf_op jit(solution)/shard_map/ppermute | solution.py:278
  17.4 0.1 collective-permute-start
  17.5 1.0 %fusion = (bf16[64,2,128]{2,1,0:T(2,128)(2,1)S(1)}, bf16[64,2,128]{2,1,0:T(2,128)(2,1)S(1)}) fusion(bf16[64,112,128]{2,1,0:T(8,128)(2,1)} %x_hbm.1), kind=kLoop, calls=%fused_computation.21 | loop fusion | bytes 131072 | tf_op jit(solution)/shard_map/slice | solution.py:315
  18.5 1.0 %collective-permute-done.1 = bf16[2,112,128]{2,1,0:T(8,128)(2,1)S(1)} collective-permute-done((bf16[2,112,128]{2,1,0:T(8,128)(2,1)S(1)}, bf16[2,112,128]{2,1,0:T(8,128)(2,1)S(1)}, u32[]{:S(2)}, u32[]{:S(2)}) %collective-permute-start.1) | collective-permute-done | bytes 57376 | tf_op jit(solution)/shard_map/ppermute | solution.py:278
  19.5 0.0 collective-permute-done
  19.5 0.0 copy-start.4
  19.6 0.0 copy-start.5
  19.6 0.0 all-to-all-done
  19.6 0.0 copy-start.6
  19.6 0.1 broadcast_select_fusion.6
  19.7 5.3 %collective-permute-start.3 = (bf16[68,2,128]{2,1,0:T(2,128)(2,1)S(1)}, bf16[68,2,128]{2,1,0:T(2,128)(2,1)S(1)}, u32[]{:S(2)}, u32[]{:S(2)}) collective-permute-start(bf16[68,2,128]{2,1,0:T(2,128)(2,1)S(1)} %get-tuple-element.67), channel_id=1, source_target_pairs={{1,2},{2,1},{3,4},{4,3},{5,6},{6,5},{7,8},{8,7},{9,10},{10,9},{11,... | collective-permute-start | bytes 104456 | tf_op jit(solution)/shard_map/ppermute | solution.py:278
  25.0 0.0 collective-permute-start.2
  25.0 1.8 %collective-permute-done.3 = bf16[68,2,128]{2,1,0:T(2,128)(2,1)S(1)} collective-permute-done((bf16[68,2,128]{2,1,0:T(2,128)(2,1)S(1)}, bf16[68,2,128]{2,1,0:T(2,128)(2,1)S(1)}, u32[]{:S(2)}, u32[]{:S(2)}) %collective-permute-start.3) | collective-permute-done | bytes 34848 | tf_op jit(solution)/shard_map/ppermute | solution.py:278
  26.8 1.4 %collective-permute-done.2 = bf16[68,2,128]{2,1,0:T(2,128)(2,1)S(1)} collective-permute-done((bf16[68,2,128]{2,1,0:T(2,128)(2,1)S(1)}, bf16[68,2,128]{2,1,0:T(2,128)(2,1)S(1)}, u32[]{:S(2)}, u32[]{:S(2)}) %collective-permute-start.2) | collective-permute-done | bytes 34848 | tf_op jit(solution)/shard_map/ppermute | solution.py:278
  28.2 6.1 %all-to-all-start.1 = ((bf16[32,128,256]{2,1,0:T(8,128)(2,1)}), bf16[32,128,256]{2,1,0:T(8,128)(2,1)S(1)}, u32[]{:S(2)}, u32[]{:S(2)}) async-start(bf16[32,128,256]{2,1,0:T(8,128)(2,1)} %bitcast.23), calls=%async_computation.1 | async-start | bytes 4194304 | tf_op jit(solution)/shard_map/all_to_all | solution.py:317
  34.3 0.0 copy-done.3
  34.3 0.1 copy.13
  34.5 0.0 copy-done.2
  34.5 0.1 copy.12
  34.6 0.7 broadcast_select_fusion.4
  35.3 0.0 copy-done.4
  35.3 0.0 copy-done.5
  35.3 0.0 copy-done.6
  35.3 19.9 %forward.1 = (f32[4096,256]{1,0:T(8,128)}, bf16[4096,512]{1,0:T(8,128)(2,1)}, f32[33,2,128,128]{3,2,1,0:T(8,128)}, bf16[1536,256]{1,0:T(8,128)(2,1)}, bf16[1536,256]{1,0:T(8,128)(2,1)}, /*index=5*/s32[4194304]{0:T(1024)}) custom-call(s32[4096]{0:T(1024)} %bitcast.26, bf16[2,112,128]{2,1,0:T(8,128)(2,1)} %copy-done.5, bf16[2,112,128]{2,1,0:T(8,128)(2,1)} %copy-done.4, ...), custom_call_target="tpu_custom_call" | custom-call | tf_op jit(solution)/shard_map/forward/pallas_call | solution.py:321
  55.2 10.2 %all-to-all-done.1 = bf16[32,128,256]{2,1,0:T(8,128)(2,1)S(1)} async-done(((bf16[32,128,256]{2,1,0:T(8,128)(2,1)}), bf16[32,128,256]{2,1,0:T(8,128)(2,1)S(1)}, u32[]{:S(2)}, u32[]{:S(2)}) %all-to-all-start.1) | async-done | bytes 2097184 | tf_op jit(solution)/shard_map/all_to_all | solution.py:317
  65.5 0.0 slice-start
  65.5 0.0 slice-start.1
  65.5 0.0 copy-start
  65.5 12.1 %scatter.1 = (f32[64,112,128]{2,1,0:T(8,128)S(1)}, bf16[2,112,128]{2,1,0:T(8,128)(2,1)S(1)}, bf16[2,112,128]{2,1,0:T(8,128)(2,1)S(1)}, bf16[64,2,128]{2,1,0:T(2,128)(2,1)S(1)}, bf16[64,2,128]{2,1,0:T(2,128)(2,1)S(1)}) custom-call(bf16[256,512]{1,0:T(8,128)(2,1)S(1)} %bitcast.19, bf16[512,128]{1,0:T(8,128)(2,1)S(1)} %bitcast.20, ...), custom_call_target="tpu_custom_call" | custom-call | tf_op jit(solution)/shard_map/scatter/pallas_call | solution.py:352
  77.7 2.5 %collective-permute-start.5 = (bf16[2,112,128]{2,1,0:T(8,128)(2,1)S(1)}, bf16[2,112,128]{2,1,0:T(8,128)(2,1)S(1)}, u32[]{:S(2)}, u32[]{:S(2)}) collective-permute-start(bf16[2,112,128]{2,1,0:T(8,128)(2,1)S(1)} %get-tuple-element.57), channel_id=1, source_target_pairs={{32,64},{64,32},{33,65},{65,33},{34,66},{66,34},{35,67},{67,35},{3... | collective-permute-start | bytes 172040 | tf_op jit(solution)/shard_map/ppermute | solution.py:278
  80.1 0.1 collective-permute-start.4
  80.2 4.4 %collective-permute-done.5 = bf16[2,112,128]{2,1,0:T(8,128)(2,1)S(1)} collective-permute-done((bf16[2,112,128]{2,1,0:T(8,128)(2,1)S(1)}, bf16[2,112,128]{2,1,0:T(8,128)(2,1)S(1)}, u32[]{:S(2)}, u32[]{:S(2)}) %collective-permute-start.5) | collective-permute-done | bytes 57376 | tf_op jit(solution)/shard_map/ppermute | solution.py:278
  84.7 0.0 collective-permute-done.4
  84.7 0.1 broadcast_select_fusion.2
  84.8 0.1 collective-permute-start.7
  84.9 0.3 collective-permute-start.6
  85.3 6.7 %collective-permute-done.7 = bf16[68,2,128]{2,1,0:T(2,128)(2,1)S(1)} collective-permute-done((bf16[68,2,128]{2,1,0:T(2,128)(2,1)S(1)}, bf16[68,2,128]{2,1,0:T(2,128)(2,1)S(1)}, u32[]{:S(2)}, u32[]{:S(2)}) %collective-permute-start.7) | collective-permute-done | bytes 34848 | tf_op jit(solution)/shard_map/ppermute | solution.py:278
  91.9 0.0 collective-permute-done.6
  92.0 0.0 slice-done
  92.0 0.0 slice-done.1
  92.0 0.0 copy-done
  92.0 0.0 copy-done.1
  92.0 8.4 %backward.1 = f32[64,112,128]{2,1,0:T(8,128)} custom-call(f32[64,112,128]{2,1,0:T(8,128)S(1)} %get-tuple-element.39.d_ref, bf16[2,112,128]{2,1,0:T(8,128)(2,1)S(1)} %get-tuple-element.56.top_ref, bf16[2,112,128]{2,1,0:T(8,128)(2,1)S(1)} %get-tuple-element.55.bottom_ref, bf16[68,2,128]{2,1,0:T(2,128)(2,1)S(1)} %bitcast.22, bf16[68,2,128]{2,1,0:T(2,128)(2,1)S(1)} %bitcast.21, ...), custom_call_target="tpu_custom_call" | custom-call | tf_op jit(solution)/shard_map/backward/pallas_call | solution.py:372
  (9 shorter events, 0.1 us)
Async XLA Ops:
  0.0 34.3 %copy-start.3 = (bf16[128,512]{1,0:T(8,128)(2,1)S(1)}, bf16[128,512]{1,0:T(8,128)(2,1)}, u32[]{:S(2)}) copy-start(bf16[128,512]{1,0:T(8,128)(2,1)} %into_hbm.1) | copy-start | bytes 393220
  0.0 34.5 %copy-start.2 = (bf16[512,256]{1,0:T(8,128)(2,1)S(1)}, bf16[512,256]{1,0:T(8,128)(2,1)}, u32[]{:S(2)}) copy-start(bf16[512,256]{1,0:T(8,128)(2,1)} %out_hbm.1) | copy-start | bytes 786436
  1.5 18.1 %all-to-all-start = ((s32[32,1,128]{2,1,0:T(1,128)}), s32[32,1,128]{2,1,0:T(1,128)S(1)}, u32[]{:S(2)}, u32[]{:S(2)}) async-start(s32[32,1,128]{2,1,0:T(1,128)} %compare_select_fusion), calls=%async_computation | async-start | bytes 32768 | tf_op jit(solution)/shard_map/all_to_all | solution.py:311
  12.2 7.3 %collective-permute-start.1 = (bf16[2,112,128]{2,1,0:T(8,128)(2,1)S(1)}, bf16[2,112,128]{2,1,0:T(8,128)(2,1)S(1)}, u32[]{:S(2)}, u32[]{:S(2)}) collective-permute-start(bf16[2,112,128]{2,1,0:T(8,128)(2,1)S(1)} %get-tuple-element.53), channel_id=1, source_target_pairs={{32,64},{64,32},{33,65},{65,33},{34,66},{66,34},{35,67},{67,35},{3... | collective-permute-start | bytes 172040 | tf_op jit(solution)/shard_map/ppermute | solution.py:278
  17.4 2.1 %collective-permute-start = (bf16[2,112,128]{2,1,0:T(8,128)(2,1)S(1)}, bf16[2,112,128]{2,1,0:T(8,128)(2,1)S(1)}, u32[]{:S(2)}, u32[]{:S(2)}) collective-permute-start(bf16[2,112,128]{2,1,0:T(8,128)(2,1)S(1)} %get-tuple-element.54), channel_id=1, source_target_pairs={{0,32},{32,0},{64,96},{96,64},{1,33},{33,1},{65,97},{97,65},{2,34}... | collective-permute-start | bytes 172040 | tf_op jit(solution)/shard_map/ppermute | solution.py:278
  19.5 15.7 %copy-start.4 = (bf16[2,112,128]{2,1,0:T(8,128)(2,1)}, bf16[2,112,128]{2,1,0:T(8,128)(2,1)S(1)}, u32[]{:S(2)}) copy-start(bf16[2,112,128]{2,1,0:T(8,128)(2,1)S(1)} %get-tuple-element.31.bottom_ref) | copy-start | bytes 172036
  19.6 15.7 %copy-start.5 = (bf16[2,112,128]{2,1,0:T(8,128)(2,1)}, bf16[2,112,128]{2,1,0:T(8,128)(2,1)S(1)}, u32[]{:S(2)}) copy-start(bf16[2,112,128]{2,1,0:T(8,128)(2,1)S(1)} %get-tuple-element.30.top_ref) | copy-start | bytes 172036
  19.6 15.7 %copy-start.6 = (s32[32,1,128]{2,1,0:T(1,128)}, s32[32,1,128]{2,1,0:T(1,128)S(1)}, u32[]{:S(2)}) copy-start(s32[32,1,128]{2,1,0:T(1,128)S(1)} %all-to-all-done) | copy-start | bytes 49156
  19.7 7.1 %collective-permute-start.3 = (bf16[68,2,128]{2,1,0:T(2,128)(2,1)S(1)}, bf16[68,2,128]{2,1,0:T(2,128)(2,1)S(1)}, u32[]{:S(2)}, u32[]{:S(2)}) collective-permute-start(bf16[68,2,128]{2,1,0:T(2,128)(2,1)S(1)} %get-tuple-element.67), channel_id=1, source_target_pairs={{1,2},{2,1},{3,4},{4,3},{5,6},{6,5},{7,8},{8,7},{9,10},{10,9},{11,... | collective-permute-start | bytes 104456 | tf_op jit(solution)/shard_map/ppermute | solution.py:278
  25.0 3.2 %collective-permute-start.2 = (bf16[68,2,128]{2,1,0:T(2,128)(2,1)S(1)}, bf16[68,2,128]{2,1,0:T(2,128)(2,1)S(1)}, u32[]{:S(2)}, u32[]{:S(2)}) collective-permute-start(bf16[68,2,128]{2,1,0:T(2,128)(2,1)S(1)} %get-tuple-element.68), channel_id=1, source_target_pairs={{0,1},{1,0},{2,3},{3,2},{4,5},{5,4},{6,7},{7,6},{8,9},{9,8},{10,11... | collective-permute-start | bytes 104456 | tf_op jit(solution)/shard_map/ppermute | solution.py:278
  28.2 37.3 %all-to-all-start.1 = ((bf16[32,128,256]{2,1,0:T(8,128)(2,1)}), bf16[32,128,256]{2,1,0:T(8,128)(2,1)S(1)}, u32[]{:S(2)}, u32[]{:S(2)}) async-start(bf16[32,128,256]{2,1,0:T(8,128)(2,1)} %bitcast.23), calls=%async_computation.1 | async-start | bytes 4194304 | tf_op jit(solution)/shard_map/all_to_all | solution.py:317
  65.5 26.5 %slice-start = ((s8[4325376]{0:T(1024)(128)(4,1)}), s8[4194304]{0:T(1024)(128)(4,1)S(1)}, s32[]{:S(2)}) async-start(s8[4325376]{0:T(1024)(128)(4,1)} %bitcast.17), calls=%async_computation.2 | async-start | bytes 8388608
  65.5 26.5 %slice-start.1 = ((s8[4325376]{0:T(1024)(128)(4,1)}), s8[131072]{0:T(1024)(128)(4,1)S(1)}, s32[]{:S(2)}) async-start(s8[4325376]{0:T(1024)(128)(4,1)} %bitcast.17), calls=%async_computation.3 | async-start | bytes 262144
  65.5 26.5 %copy-start = (bf16[1536,256]{1,0:T(8,128)(2,1)S(1)}, bf16[1536,256]{1,0:T(8,128)(2,1)}, u32[]{:S(2)}) copy-start(bf16[1536,256]{1,0:T(8,128)(2,1)} %get-tuple-element.48.weights_one) | copy-start | bytes 2359300
  65.5 26.5 %copy-start.1 = (bf16[1536,256]{1,0:T(8,128)(2,1)S(1)}, bf16[1536,256]{1,0:T(8,128)(2,1)}, u32[]{:S(2)}) copy-start(bf16[1536,256]{1,0:T(8,128)(2,1)} %get-tuple-element.49.weights_two) | copy-start | bytes 2359300
  77.7 7.0 %collective-permute-start.5 = (bf16[2,112,128]{2,1,0:T(8,128)(2,1)S(1)}, bf16[2,112,128]{2,1,0:T(8,128)(2,1)S(1)}, u32[]{:S(2)}, u32[]{:S(2)}) collective-permute-start(bf16[2,112,128]{2,1,0:T(8,128)(2,1)S(1)} %get-tuple-element.57), channel_id=1, source_target_pairs={{32,64},{64,32},{33,65},{65,33},{34,66},{66,34},{35,67},{67,35},{3... | collective-permute-start | bytes 172040 | tf_op jit(solution)/shard_map/ppermute | solution.py:278
  80.1 4.5 %collective-permute-start.4 = (bf16[2,112,128]{2,1,0:T(8,128)(2,1)S(1)}, bf16[2,112,128]{2,1,0:T(8,128)(2,1)S(1)}, u32[]{:S(2)}, u32[]{:S(2)}) collective-permute-start(bf16[2,112,128]{2,1,0:T(8,128)(2,1)S(1)} %get-tuple-element.58), channel_id=1, source_target_pairs={{0,32},{32,0},{64,96},{96,64},{1,33},{33,1},{65,97},{97,65},{2,34}... | collective-permute-start | bytes 172040 | tf_op jit(solution)/shard_map/ppermute | solution.py:278
  84.8 7.1 %collective-permute-start.7 = (bf16[68,2,128]{2,1,0:T(2,128)(2,1)S(1)}, bf16[68,2,128]{2,1,0:T(2,128)(2,1)S(1)}, u32[]{:S(2)}, u32[]{:S(2)}) collective-permute-start(bf16[68,2,128]{2,1,0:T(2,128)(2,1)S(1)} %get-tuple-element.63), channel_id=1, source_target_pairs={{1,2},{2,1},{3,4},{4,3},{5,6},{6,5},{7,8},{8,7},{9,10},{10,9},{11,... | collective-permute-start | bytes 104456 | tf_op jit(solution)/shard_map/ppermute | solution.py:278
  84.9 7.0 %collective-permute-start.6 = (bf16[68,2,128]{2,1,0:T(2,128)(2,1)S(1)}, bf16[68,2,128]{2,1,0:T(2,128)(2,1)S(1)}, u32[]{:S(2)}, u32[]{:S(2)}) collective-permute-start(bf16[68,2,128]{2,1,0:T(2,128)(2,1)S(1)} %get-tuple-element.64), channel_id=1, source_target_pairs={{0,1},{1,0},{2,3},{3,2},{4,5},{5,4},{6,7},{7,6},{8,9},{9,8},{10,11... | collective-permute-start | bytes 104456 | tf_op jit(solution)/shard_map/ppermute | solution.py:278

commit v3 on v2

--- a/solution.py
+++ b/solution.py
@@ -78,11 +78,12 @@
 def pad_rim(padded_ref, top_ref, bottom_ref, left_ref, right_ref):
     pairs = padded_ref.shape[0]
     width = top_ref.shape[1]
-    padded_ref[0, :, 8 : 8 + width, :] = top_ref[...].astype(F32)
-    padded_ref[pairs - 1, :, 8 : 8 + width, :] = bottom_ref[...].astype(F32)
-    padded_ref[:, :, 6:8, :] = left_ref[...].astype(F32).reshape(pairs, 2, 2, -1)
-    padded_ref[:, :, 8 + width : 10 + width, :] = right_ref[...].astype(F32).reshape(
-        pairs, 2, 2, -1
+    padded_ref[0, :, 6 : 6 + width, :] = top_ref[...].astype(F32)
+    padded_ref[pairs - 1, :, 6 : 6 + width, :] = bottom_ref[...].astype(F32)
+    sides = (pairs - 2, 2, 2, padded_ref.shape[-1])
+    padded_ref[1 : pairs - 1, :, 6:8, :] = left_ref[...].astype(F32).reshape(sides)
+    padded_ref[1 : pairs - 1, :, 4 + width : 6 + width, :] = right_ref[...].astype(F32).reshape(
+        sides
     )
 
 
@@ -282,18 +283,17 @@
     even = lax.rem(lax.axis_index(axis), 2) == 0
     one = swapped(jnp.where(even, high, low), axis, 0, around)
     two = swapped(jnp.where(even, low, high), axis, 1, around)
-    one, two, after = lax.optimization_barrier((one, two, after))
+    two, after = lax.optimization_barrier((two, after))
     return (jnp.where(even, two, one), jnp.where(even, one, two)), after
 
 
-def rows_around(head, tail):
-    return neighbours(head, tail, "lat", False)[0]
-
-
-def columns_around(top, bottom, left, right, after=()):
-    left = jnp.concatenate([top[:, :2], left, bottom[:, :2]], axis=0)
-    right = jnp.concatenate([top[:, -2:], right, bottom[:, -2:]], axis=0)
-    return neighbours(left, right, "lon", True, after)
+def ring_around(head, tail, left, right, beside=(), after=()):
+    (left, right), _ = neighbours(left, right, "lon", True)
+    left, right, beside = lax.optimization_barrier((left, right, beside))
+    head = jnp.concatenate([left[:2], head, right[:2]], axis=1)
+    tail = jnp.concatenate([left[-2:], tail, right[-2:]], axis=1)
+    (top, bottom), after = neighbours(head, tail, "lat", False, after)
+    return (top, bottom, left, right), beside, after
 
 
 def per_device(
@@ -310,10 +310,9 @@
     cells = jnp.where(live, columns[0], rows * width)
     cells = lax.all_to_all(cells, "lon", 0, 0, tiled=True).reshape(-1)
     x = starting_vector
-    top, bottom = rows_around(x[:2], x[-2:])
-    top, bottom, cells = lax.optimization_barrier((top, bottom, cells))
-    sides, radiance = columns_around(top, bottom, x[:, :2], x[:, -2:], innovations[0])
-    ring = (top, bottom, *sides)
+    ring, cells, radiance = ring_around(
+        x[:2], x[-2:], x[:, :2], x[:, -2:], cells, innovations[0]
+    )
     radiance = lax.all_to_all(radiance, "lon", 0, 0, tiled=True).reshape(taken, channels)
 
     weights = jax.ShapeDtypeStruct((12 * depth, 2 * depth), BF)
@@ -367,8 +366,7 @@
         name="scatter",
     )(obs_out.T, obs_in.T, radiance, predicted, z_slope, cells)
 
-    top, bottom = rows_around(head, tail)
-    ring = (top, bottom, *columns_around(top, bottom, left, right)[0])
+    ring, _, _ = ring_around(head, tail, left, right)
     return pl.pallas_call(
         backward_kernel,
         out_shape=jax.ShapeDtypeStruct((rows, width, depth), F32),

time: 101 us -> 98.7 us (0.977)
  waiting for transfers between devices: 25.5 us -> 20.7 us
  starting transfers between devices: 29.5 us -> 32 us
    all_to_all x1, waiting for transfers between devices: 10.2 us -> 5.91 us  [per_device(): lax.all_to_all(radiance, 'lon', 0, 0, tiled=True).reshape(taken, channels)]
    ppermute x8, starting transfers between devices: 13.5 us -> 16.6 us  [swapped(): lax.ppermute(array, axis, [way for i, j in pairs for way in ((i, j), (j,...]
where the time goes in v3:
time: 98.7 us; the launch traced here: 98.4 us
  Pallas kernels  40.7 us (41%)
  starting transfers between devices  32 us (32%)
  waiting for transfers between devices  20.7 us (21%)
  other arithmetic  3.34 us (3%)
  local copies, waits for them, and re-layouts  1.17 us (1%)
    pallas_call x1, Pallas kernels, per_device(): pl.pallas_call(forward_kernel, out_shape=(jax.ShapeDtypeStruct((taken, ch...  19.9 us
    ppermute x8, starting transfers between devices, swapped(): lax.ppermute(array, axis, [way for i, j in pairs for way in ((i, j), (j,...  16.6 us
    ppermute x8, waiting for transfers between devices, swapped(): lax.ppermute(array, axis, [way for i, j in pairs for way in ((i, j), (j,...  14.8 us
    pallas_call x1, Pallas kernels, per_device(): pl.pallas_call(scatter_kernel, out_shape=(jax.ShapeDtypeStruct((rows, wid...  12.3 us
    all_to_all x1, starting transfers between devices, per_device(): cells = lax.all_to_all(cells, 'lon', 0, 0, tiled=True).reshape(-1)  9.81 us
    pallas_call x1, Pallas kernels, per_device(): pl.pallas_call(backward_kernel, out_shape=jax.ShapeDtypeStruct((rows, wid...  8.4 us
    all_to_all x1, waiting for transfers between devices, per_device(): lax.all_to_all(radiance, 'lon', 0, 0, tiled=True).reshape(taken, channels)  5.91 us
    all_to_all x1, starting transfers between devices, per_device(): lax.all_to_all(radiance, 'lon', 0, 0, tiled=True).reshape(taken, channels)  5.65 us
  transfers between devices with their start and end apart: 10, of which 6 were waited for; matrix products, arithmetic and copies ran while one was open for 3% of the time, Pallas kernels for 20%

profile of v3, /device:TPU:1, one launch (start us, length us, event | category | flops | bytes accessed | tf_op | source)
XLA Modules:
  0.0 98.4 jit_solution(4581354792076499908)
XLA Ops:
  0.0 0.0 copy-start.3
  0.0 0.0 copy-start.2
  0.0 1.5 %compare_select_fusion = s32[32,1,128]{2,1,0:T(1,128)} fusion(s32[32,1,128]{2,1,0:T(1,128)} %bitcast.43, s32[32]{0:T(128)} %bitcast.45), kind=kLoop, calls=%fused_computation | loop fusion | flops 8192 | bytes 32896 | tf_op jit(solution)/shard_map/jit(_where)/select_n | solution.py:310
  1.5 9.8 %all-to-all-start = ((s32[32,1,128]{2,1,0:T(1,128)}), s32[32,1,128]{2,1,0:T(1,128)S(1)}, u32[]{:S(2)}, u32[]{:S(2)}) async-start(s32[32,1,128]{2,1,0:T(1,128)} %compare_select_fusion), calls=%async_computation | async-start | bytes 32768 | tf_op jit(solution)/shard_map/all_to_all | solution.py:311
  11.3 1.1 %broadcast_select_fusion.6 = (bf16[64,2,128]{2,1,0:T(2,128)(2,1)S(1)}, bf16[64,2,128]{2,1,0:T(2,128)(2,1)S(1)}) fusion(pred[]{:T(512)S(6)} %eq.9, bf16[64,112,128]{2,1,0:T(8,128)(2,1)} %x_hbm.1), kind=kLoop, calls=%fused_computation.7 | loop fusion | flops 32768 | bytes 131073 | tf_op jit(solution)/shard_map/jit(_where)/select_n | solution.py:284
  12.4 1.3 %collective-permute-start.1 = (bf16[64,2,128]{2,1,0:T(2,128)(2,1)S(1)}, bf16[64,2,128]{2,1,0:T(2,128)(2,1)S(1)}, u32[]{:S(2)}, u32[]{:S(2)}) collective-permute-start(bf16[64,2,128]{2,1,0:T(2,128)(2,1)S(1)} %get-tuple-element.43), channel_id=1, source_target_pairs={{0,1},{1,0},{2,3},{3,2},{4,5},{5,4},{6,7},{7,6},{8,9},{9,8},{10,11... | collective-permute-start | bytes 98312 | tf_op jit(solution)/shard_map/ppermute | solution.py:279
  13.7 4.6 %collective-permute-start = (bf16[64,2,128]{2,1,0:T(2,128)(2,1)S(1)}, bf16[64,2,128]{2,1,0:T(2,128)(2,1)S(1)}, u32[]{:S(2)}, u32[]{:S(2)}) collective-permute-start(bf16[64,2,128]{2,1,0:T(2,128)(2,1)S(1)} %get-tuple-element.44), channel_id=1, source_target_pairs={{1,2},{2,1},{3,4},{4,3},{5,6},{6,5},{7,8},{8,7},{9,10},{10,9},{11,... | collective-permute-start | bytes 98312 | tf_op jit(solution)/shard_map/ppermute | solution.py:279
  18.3 0.9 fusion
  19.1 1.5 %collective-permute-done = bf16[64,2,128]{2,1,0:T(2,128)(2,1)S(1)} collective-permute-done((bf16[64,2,128]{2,1,0:T(2,128)(2,1)S(1)}, bf16[64,2,128]{2,1,0:T(2,128)(2,1)S(1)}, u32[]{:S(2)}, u32[]{:S(2)}) %collective-permute-start) | collective-permute-done | bytes 32800 | tf_op jit(solution)/shard_map/ppermute | solution.py:279
  20.7 0.0 collective-permute-done.1
  20.7 0.0 copy-start.4
  20.7 0.0 copy-start.5
  20.7 0.0 all-to-all-done
  20.7 0.0 copy-start.6
  20.7 0.1 broadcast_select_fusion.14
  20.8 6.9 %collective-permute-start.2 = (bf16[2,116,128]{2,1,0:T(8,128)(2,1)S(1)}, bf16[2,116,128]{2,1,0:T(8,128)(2,1)S(1)}, u32[]{:S(2)}, u32[]{:S(2)}) collective-permute-start(bf16[2,116,128]{2,1,0:T(8,128)(2,1)S(1)} %get-tuple-element.52), channel_id=1, source_target_pairs={{32,64},{64,32},{33,65},{65,33},{34,66},{66,34},{35,67},{67,35},{3... | collective-permute-start | bytes 178184 | tf_op jit(solution)/shard_map/ppermute | solution.py:279
  27.7 1.9 %collective-permute-done.2 = bf16[2,116,128]{2,1,0:T(8,128)(2,1)S(1)} collective-permute-done((bf16[2,116,128]{2,1,0:T(8,128)(2,1)S(1)}, bf16[2,116,128]{2,1,0:T(8,128)(2,1)S(1)}, u32[]{:S(2)}, u32[]{:S(2)}) %collective-permute-start.2) | collective-permute-done | bytes 59424 | tf_op jit(solution)/shard_map/ppermute | solution.py:279
  29.6 5.7 %all-to-all-start.1 = ((bf16[32,128,256]{2,1,0:T(8,128)(2,1)}), bf16[32,128,256]{2,1,0:T(8,128)(2,1)S(1)}, u32[]{:S(2)}, u32[]{:S(2)}) async-start(bf16[32,128,256]{2,1,0:T(8,128)(2,1)} %bitcast.31), calls=%async_computation.1 | async-start | bytes 4194304 | tf_op jit(solution)/shard_map/all_to_all | solution.py:316
  35.3 0.1 collective-permute-start.3
  35.3 0.0 copy-done.3
  35.4 0.1 copy.13
  35.5 0.0 copy-done.2
  35.5 0.1 copy.12
  35.6 0.9 collective-permute-done.3
  36.6 0.7 broadcast_select_fusion.12
  37.2 0.0 copy-done.4
  37.2 0.0 copy-done.5
  37.2 0.0 copy-done.6
  37.3 19.9 %forward.1 = (f32[4096,256]{1,0:T(8,128)}, bf16[4096,512]{1,0:T(8,128)(2,1)}, f32[33,2,128,128]{3,2,1,0:T(8,128)}, bf16[1536,256]{1,0:T(8,128)(2,1)}, bf16[1536,256]{1,0:T(8,128)(2,1)}, /*index=5*/s32[4194304]{0:T(1024)}) custom-call(s32[4096]{0:T(1024)} %bitcast.36, bf16[2,116,128]{2,1,0:T(8,128)(2,1)} %get-tuple-element.48.top_ref, ...), custom_call_target="tpu_custom_call" | custom-call | tf_op jit(solution)/shard_map/forward/pallas_call | solution.py:320
  57.2 5.9 %all-to-all-done.1 = bf16[32,128,256]{2,1,0:T(8,128)(2,1)S(1)} async-done(((bf16[32,128,256]{2,1,0:T(8,128)(2,1)}), bf16[32,128,256]{2,1,0:T(8,128)(2,1)S(1)}, u32[]{:S(2)}, u32[]{:S(2)}) %all-to-all-start.1) | async-done | bytes 2097184 | tf_op jit(solution)/shard_map/all_to_all | solution.py:316
  63.1 0.0 slice-start
  63.1 0.0 slice-start.1
  63.1 0.0 copy-start
  63.1 12.3 %scatter.1 = (f32[64,112,128]{2,1,0:T(8,128)S(1)}, bf16[2,112,128]{2,1,0:T(8,128)(2,1)S(1)}, bf16[2,112,128]{2,1,0:T(8,128)(2,1)S(1)}, bf16[64,2,128]{2,1,0:T(2,128)(2,1)S(1)}, bf16[64,2,128]{2,1,0:T(2,128)(2,1)S(1)}) custom-call(bf16[256,512]{1,0:T(8,128)(2,1)S(1)} %bitcast.23, bf16[512,128]{1,0:T(8,128)(2,1)S(1)} %bitcast.24, ...), custom_call_target="tpu_custom_call" | custom-call | tf_op jit(solution)/shard_map/scatter/pallas_call | solution.py:351
  75.5 0.1 collective-permute-start.4
  75.6 0.1 collective-permute-start.5
  75.7 6.9 %collective-permute-done.4 = bf16[64,2,128]{2,1,0:T(2,128)(2,1)S(1)} collective-permute-done((bf16[64,2,128]{2,1,0:T(2,128)(2,1)S(1)}, bf16[64,2,128]{2,1,0:T(2,128)(2,1)S(1)}, u32[]{:S(2)}, u32[]{:S(2)}) %collective-permute-start.4) | collective-permute-done | bytes 32800 | tf_op jit(solution)/shard_map/ppermute | solution.py:279
  82.6 0.0 collective-permute-done.5
  82.6 0.1 broadcast_select_fusion.10
  82.7 3.2 %collective-permute-start.6 = (bf16[2,116,128]{2,1,0:T(8,128)(2,1)S(1)}, bf16[2,116,128]{2,1,0:T(8,128)(2,1)S(1)}, u32[]{:S(2)}, u32[]{:S(2)}) collective-permute-start(bf16[2,116,128]{2,1,0:T(8,128)(2,1)S(1)} %get-tuple-element.50), channel_id=1, source_target_pairs={{32,64},{64,32},{33,65},{65,33},{34,66},{66,34},{35,67},{67,35},{3... | collective-permute-start | bytes 178184 | tf_op jit(solution)/shard_map/ppermute | solution.py:279
  85.9 0.3 collective-permute-start.7
  86.2 3.5 %collective-permute-done.6 = bf16[2,116,128]{2,1,0:T(8,128)(2,1)S(1)} collective-permute-done((bf16[2,116,128]{2,1,0:T(8,128)(2,1)S(1)}, bf16[2,116,128]{2,1,0:T(8,128)(2,1)S(1)}, u32[]{:S(2)}, u32[]{:S(2)}) %collective-permute-start.6) | collective-permute-done | bytes 59424 | tf_op jit(solution)/shard_map/ppermute | solution.py:279
  89.7 0.0 collective-permute-done.7
  89.7 0.0 slice-done
  89.7 0.0 slice-done.1
  89.7 0.0 copy-done
  89.8 0.0 copy-done.1
  89.8 8.4 %backward.1 = f32[64,112,128]{2,1,0:T(8,128)} custom-call(f32[64,112,128]{2,1,0:T(8,128)S(1)} %get-tuple-element.31.d_ref, bf16[2,116,128]{2,1,0:T(8,128)(2,1)S(1)} %get-tuple-element.46.top_ref, bf16[2,116,128]{2,1,0:T(8,128)(2,1)S(1)} %get-tuple-element.45.bottom_ref, bf16[64,2,128]{2,1,0:T(2,128)(2,1)S(1)} %bitcast.28, bf16[64,2,128]{2,1,0:T(2,128)(2,1)S(1)} %bitcast.26, ...), custom_call_target="tpu_custom_call" | custom-call | tf_op jit(solution)/shard_map/backward/pallas_call | solution.py:370
  (9 shorter events, 0.1 us)
Async XLA Ops:
  0.0 35.3 %copy-start.3 = (bf16[128,512]{1,0:T(8,128)(2,1)S(1)}, bf16[128,512]{1,0:T(8,128)(2,1)}, u32[]{:S(2)}) copy-start(bf16[128,512]{1,0:T(8,128)(2,1)} %into_hbm.1) | copy-start | bytes 393220
  0.0 35.5 %copy-start.2 = (bf16[512,256]{1,0:T(8,128)(2,1)S(1)}, bf16[512,256]{1,0:T(8,128)(2,1)}, u32[]{:S(2)}) copy-start(bf16[512,256]{1,0:T(8,128)(2,1)} %out_hbm.1) | copy-start | bytes 786436
  1.5 19.2 %all-to-all-start = ((s32[32,1,128]{2,1,0:T(1,128)}), s32[32,1,128]{2,1,0:T(1,128)S(1)}, u32[]{:S(2)}, u32[]{:S(2)}) async-start(s32[32,1,128]{2,1,0:T(1,128)} %compare_select_fusion), calls=%async_computation | async-start | bytes 32768 | tf_op jit(solution)/shard_map/all_to_all | solution.py:311
  12.4 8.3 %collective-permute-start.1 = (bf16[64,2,128]{2,1,0:T(2,128)(2,1)S(1)}, bf16[64,2,128]{2,1,0:T(2,128)(2,1)S(1)}, u32[]{:S(2)}, u32[]{:S(2)}) collective-permute-start(bf16[64,2,128]{2,1,0:T(2,128)(2,1)S(1)} %get-tuple-element.43), channel_id=1, source_target_pairs={{0,1},{1,0},{2,3},{3,2},{4,5},{5,4},{6,7},{7,6},{8,9},{9,8},{10,11... | collective-permute-start | bytes 98312 | tf_op jit(solution)/shard_map/ppermute | solution.py:279
  13.7 7.0 %collective-permute-start = (bf16[64,2,128]{2,1,0:T(2,128)(2,1)S(1)}, bf16[64,2,128]{2,1,0:T(2,128)(2,1)S(1)}, u32[]{:S(2)}, u32[]{:S(2)}) collective-permute-start(bf16[64,2,128]{2,1,0:T(2,128)(2,1)S(1)} %get-tuple-element.44), channel_id=1, source_target_pairs={{1,2},{2,1},{3,4},{4,3},{5,6},{6,5},{7,8},{8,7},{9,10},{10,9},{11,... | collective-permute-start | bytes 98312 | tf_op jit(solution)/shard_map/ppermute | solution.py:279
  20.7 16.6 %copy-start.4 = (bf16[16,8,128]{2,1,0:T(8,128)(2,1)}, bf16[16,8,128]{2,1,0:T(8,128)(2,1)S(1)}, u32[]{:S(2)}) copy-start(bf16[16,8,128]{2,1,0:T(8,128)(2,1)S(1)} %get-tuple-element.69) | copy-start | bytes 98308
  20.7 16.6 %copy-start.5 = (bf16[16,8,128]{2,1,0:T(8,128)(2,1)}, bf16[16,8,128]{2,1,0:T(8,128)(2,1)S(1)}, u32[]{:S(2)}) copy-start(bf16[16,8,128]{2,1,0:T(8,128)(2,1)S(1)} %get-tuple-element.70) | copy-start | bytes 98308
  20.7 16.5 %copy-start.6 = (s32[32,1,128]{2,1,0:T(1,128)}, s32[32,1,128]{2,1,0:T(1,128)S(1)}, u32[]{:S(2)}) copy-start(s32[32,1,128]{2,1,0:T(1,128)S(1)} %all-to-all-done) | copy-start | bytes 49156
  20.8 8.8 %collective-permute-start.2 = (bf16[2,116,128]{2,1,0:T(8,128)(2,1)S(1)}, bf16[2,116,128]{2,1,0:T(8,128)(2,1)S(1)}, u32[]{:S(2)}, u32[]{:S(2)}) collective-permute-start(bf16[2,116,128]{2,1,0:T(8,128)(2,1)S(1)} %get-tuple-element.52), channel_id=1, source_target_pairs={{32,64},{64,32},{33,65},{65,33},{34,66},{66,34},{35,67},{67,35},{3... | collective-permute-start | bytes 178184 | tf_op jit(solution)/shard_map/ppermute | solution.py:279
  29.6 33.5 %all-to-all-start.1 = ((bf16[32,128,256]{2,1,0:T(8,128)(2,1)}), bf16[32,128,256]{2,1,0:T(8,128)(2,1)S(1)}, u32[]{:S(2)}, u32[]{:S(2)}) async-start(bf16[32,128,256]{2,1,0:T(8,128)(2,1)} %bitcast.31), calls=%async_computation.1 | async-start | bytes 4194304 | tf_op jit(solution)/shard_map/all_to_all | solution.py:316
  35.3 1.3 %collective-permute-start.3 = (bf16[2,116,128]{2,1,0:T(8,128)(2,1)S(1)}, bf16[2,116,128]{2,1,0:T(8,128)(2,1)S(1)}, u32[]{:S(2)}, u32[]{:S(2)}) collective-permute-start(bf16[2,116,128]{2,1,0:T(8,128)(2,1)S(1)} %get-tuple-element.51), channel_id=1, source_target_pairs={{0,32},{32,0},{64,96},{96,64},{1,33},{33,1},{65,97},{97,65},{2,34}... | collective-permute-start | bytes 178184 | tf_op jit(solution)/shard_map/ppermute | solution.py:279
  63.1 26.6 %slice-start = ((s8[4325376]{0:T(1024)(128)(4,1)}), s8[4194304]{0:T(1024)(128)(4,1)S(1)}, s32[]{:S(2)}) async-start(s8[4325376]{0:T(1024)(128)(4,1)} %bitcast.21), calls=%async_computation.2 | async-start | bytes 8388608
  63.1 26.6 %slice-start.1 = ((s8[4325376]{0:T(1024)(128)(4,1)}), s8[131072]{0:T(1024)(128)(4,1)S(1)}, s32[]{:S(2)}) async-start(s8[4325376]{0:T(1024)(128)(4,1)} %bitcast.21), calls=%async_computation.3 | async-start | bytes 262144
  63.1 26.6 %copy-start = (bf16[1536,256]{1,0:T(8,128)(2,1)S(1)}, bf16[1536,256]{1,0:T(8,128)(2,1)}, u32[]{:S(2)}) copy-start(bf16[1536,256]{1,0:T(8,128)(2,1)} %get-tuple-element.38.weights_one) | copy-start | bytes 2359300
  63.1 26.6 %copy-start.1 = (bf16[1536,256]{1,0:T(8,128)(2,1)S(1)}, bf16[1536,256]{1,0:T(8,128)(2,1)}, u32[]{:S(2)}) copy-start(bf16[1536,256]{1,0:T(8,128)(2,1)} %get-tuple-element.39.weights_two) | copy-start | bytes 2359300
  75.5 7.1 %collective-permute-start.4 = (bf16[64,2,128]{2,1,0:T(2,128)(2,1)S(1)}, bf16[64,2,128]{2,1,0:T(2,128)(2,1)S(1)}, u32[]{:S(2)}, u32[]{:S(2)}) collective-permute-start(bf16[64,2,128]{2,1,0:T(2,128)(2,1)S(1)} %bitcast.42), channel_id=1, source_target_pairs={{1,2},{2,1},{3,4},{4,3},{5,6},{6,5},{7,8},{8,7},{9,10},{10,9},{11,... | collective-permute-start | bytes 98312 | tf_op jit(solution)/shard_map/ppermute | solution.py:279
  75.6 7.0 %collective-permute-start.5 = (bf16[64,2,128]{2,1,0:T(2,128)(2,1)S(1)}, bf16[64,2,128]{2,1,0:T(2,128)(2,1)S(1)}, u32[]{:S(2)}, u32[]{:S(2)}) collective-permute-start(bf16[64,2,128]{2,1,0:T(2,128)(2,1)S(1)} %bitcast.40), channel_id=1, source_target_pairs={{0,1},{1,0},{2,3},{3,2},{4,5},{5,4},{6,7},{7,6},{8,9},{9,8},{10,11... | collective-permute-start | bytes 98312 | tf_op jit(solution)/shard_map/ppermute | solution.py:279
  82.7 7.0 %collective-permute-start.6 = (bf16[2,116,128]{2,1,0:T(8,128)(2,1)S(1)}, bf16[2,116,128]{2,1,0:T(8,128)(2,1)S(1)}, u32[]{:S(2)}, u32[]{:S(2)}) collective-permute-start(bf16[2,116,128]{2,1,0:T(8,128)(2,1)S(1)} %get-tuple-element.50), channel_id=1, source_target_pairs={{32,64},{64,32},{33,65},{65,33},{34,66},{66,34},{35,67},{67,35},{3... | collective-permute-start | bytes 178184 | tf_op jit(solution)/shard_map/ppermute | solution.py:279
  85.9 3.8 %collective-permute-start.7 = (bf16[2,116,128]{2,1,0:T(8,128)(2,1)S(1)}, bf16[2,116,128]{2,1,0:T(8,128)(2,1)S(1)}, u32[]{:S(2)}, u32[]{:S(2)}) collective-permute-start(bf16[2,116,128]{2,1,0:T(8,128)(2,1)S(1)} %get-tuple-element.49), channel_id=1, source_target_pairs={{0,32},{32,0},{64,96},{96,64},{1,33},{33,1},{65,97},{97,65},{2,34}... | collective-permute-start | bytes 178184 | tf_op jit(solution)/shard_map/ppermute | solution.py:279
